TPU v7x, 512 devices: a whole 4x4x16 slice. The times are simulated.
512 devices in a mesh: fsdp: 16 (over x, z_hi, core), frame: 32 (over y, z_lo).
Axes of the slice: x: 4, y: 4, z: 16 (z_hi: 2, z_lo: 8; z = z_hi * 8 + z_lo), core: 2. Of those that a mesh axis runs over, the one named last changes fastest.
Arguments:
- temporal_out: bfloat16 [32768, 4096], P('frame', 'fsdp'), may hold values from -6 to 6
- norm_gain: bfloat16 [4096], P('fsdp'), may hold values from 0.25 to 1.75
- input_proj: bfloat16 [4096, 1024], P('fsdp'), may hold values from -0.09375 to 0.09375
- code_table: bfloat16 [1024, 1024], P('fsdp'), may hold values from -6 to 6
- depth_gain: bfloat16 [1024], replicated, may hold values from 0.25 to 1.75
- depth_proj: bfloat16 [1024, 3072], P('frame'), may hold values from -0.1875 to 0.1875
- depth_out: bfloat16 [1024, 1024], replicated, may hold values from -0.1875 to 0.1875
- code_ids: int32 [32, 16, 64, 8], P('frame', 'fsdp'), may hold values from 0 to 1023
Outputs:
- depth_stream: bfloat16 [32, 16, 64, 8, 1024], P('frame', 'fsdp')
All inputs are finite; a program needn't handle non-finite values.
Results may differ from a plain program's by a relative error of at most 0.014.
Values may be sent and summed in bfloat16 or wider, within the bound.
A program may use at most 64 MiB of HBM per device.

v0:
```python
import jax
import jax.numpy as jnp
from jax import lax
from jax.sharding import PartitionSpec as P

HEADS = 16
HEAD = 64
CODEBOOKS = 8


def per_device(
    temporal_out, norm_gain, input_proj, code_table, depth_gain, depth_proj, depth_out, code_ids
):
    groups = lax.axis_size("fsdp")
    block_len = temporal_out.shape[0]
    my_count = block_len // groups
    width = input_proj.shape[1]
    my_frames = lax.all_to_all(temporal_out, "fsdp", split_axis=0, concat_axis=1, tiled=True)
    wide = my_frames.astype(jnp.float32)
    inv_rms = lax.rsqrt(jnp.mean(wide * wide, axis=1) + 1e-05)
    rows_part = lax.all_gather(input_proj, "fsdp", axis=0, tiled=True)
    gain_part = lax.all_gather(norm_gain, "fsdp", axis=0, tiled=True)
    columns = wide
    scaled = (columns * gain_part.astype(jnp.float32)).astype(jnp.bfloat16)
    projected = jnp.dot(scaled, rows_part, preferred_element_type=jnp.float32)
    context = (projected * inv_rms[:, None]).astype(jnp.bfloat16)
    codes = code_ids.reshape(my_count, CODEBOOKS)
    piece = lax.all_gather(code_table, "fsdp", axis=0, tiled=True)
    inside = (codes >= 0) & (codes < piece.shape[0])
    found = jnp.take(piece, jnp.clip(codes, 0, piece.shape[0] - 1), axis=0)
    embedded = jnp.where(inside[..., None], found, jnp.zeros_like(found))
    stream = context.astype(jnp.float32)[:, None, :] + embedded.astype(jnp.float32)
    inv_depth = lax.rsqrt(jnp.mean(stream * stream, axis=-1, keepdims=True) + 1e-05)
    normed = (
        (stream * inv_depth * depth_gain.astype(jnp.float32))
        .astype(jnp.bfloat16)
        .reshape(-1, width)
    )
    columns = normed
    qkv = jnp.dot(
        columns,
        lax.all_gather(depth_proj, "frame", axis=0, tiled=True),
        preferred_element_type=jnp.float32,
    ).astype(jnp.bfloat16)
    qkv = qkv.reshape(my_count, CODEBOOKS, 3, HEADS, HEAD)
    queries = qkv[:, :, 0]
    keys = qkv[:, :, 1]
    values = qkv[:, :, 2]
    scores = jnp.einsum(
        "fqhd,fkhd->fhqk", queries, keys, preferred_element_type=jnp.float32
    ) / jnp.sqrt(jnp.float32(HEAD))
    causal = jnp.arange(CODEBOOKS)[:, None] >= jnp.arange(CODEBOOKS)[None, :]
    scores = jnp.where(causal, scores, jnp.float32(-1e30))
    weights = jax.nn.softmax(scores, axis=-1).astype(jnp.bfloat16)
    mixed = jnp.einsum(
        "fhqk,fkhd->fqhd", weights, values, preferred_element_type=jnp.float32
    ).astype(jnp.bfloat16)
    update = jnp.dot(mixed.reshape(-1, width), depth_out, preferred_element_type=jnp.float32)
    result = (stream.reshape(-1, width) + update).astype(jnp.bfloat16)
    return result.reshape(1, 1, my_count, CODEBOOKS, width)


def solution(mesh):
    placed = (
        P("frame", "fsdp"),
        P("fsdp"),
        P("fsdp", None),
        P("fsdp", None),
        P(),
        P("frame", None),
        P(),
        P("frame", "fsdp", None, None),
    )
    return jax.shard_map(
        per_device,
        mesh=mesh,
        in_specs=placed,
        out_specs=P("frame", "fsdp", None, None, None),
        check_vma=False,
    )
```

profile of v0, /device:TPU:4, one launch (start us, length us, event | category | flops | bytes accessed | tf_op | source)
XLA Modules:
  0.0 589.9 jit_solution(15162680901759531987)
XLA Ops:
  6.5 0.0 copy-start
  6.5 0.0 copy-start.5
  6.5 0.0 copy-start.6
  6.5 0.0 all-gather.7.cloned.1.call-start
  6.5 0.7 all-gather.7.cloned.1.call-update
  7.3 0.0 all-gather.5.cloned.1.call-start
  7.3 0.7 all-gather.5.cloned.1.call-update
  8.0 0.0 all-gather.9.cloned.1.call-start
  8.1 0.7 all-gather.9.cloned.1.call-update
  8.7 18.1 %all-to-all-start = ((bf16[16,64,256]{2,1,0:T(8,128)(2,1)}), bf16[16,64,256]{2,1,0:T(8,128)(2,1)S(1)}, u32[]{:S(2)}, u32[]{:S(2)}) async-start(bf16[16,64,256]{2,1,0:T(8,128)(2,1)} %bitcast.58), calls=%async_computation | async-start | bytes 1048576 | tf_op jit(solution)/shard_map/all_to_all | solution.py:18
  26.8 0.7 reshape.124
  27.5 46.0 %all-gather = bf16[16,1,256]{2,1,0:T(2,128)(2,1)S(1)} all-gather(bf16[1,1,256]{2,1,0:T(2,128)(2,1)S(1)} %reshape.124), channel_id=1, replica_groups=mesh['fsdp'=16,'frame'=32] {'fsdp'}, dimensions={0}, use_global_device_ids=true | all-gather | bytes 8704 | tf_op jit(solution)/shard_map/all_gather | solution.py:22
  73.5 0.7 compare_select_fusion.1
  74.2 0.1 copy.40
  74.3 0.1 reshape.116
  74.4 0.7 fusion.27
  75.1 0.1 copy.41
  75.2 0.7 compare_and_fusion
  75.9 0.1 copy.42
  76.0 0.7 broadcast_clamp_fusion
  76.7 0.1 copy.39
  76.7 0.1 min.20
  76.8 0.0 copy-done.5
  76.9 0.1 copy.38
  77.0 0.1 and.25
  77.1 0.0 copy-done.6
  77.1 0.0 all-to-all-done
  77.1 0.0 copy-start.1
  77.1 0.8 copy-done.1
  77.9 0.1 convert_bitcast_fusion.1
  78.0 0.0 copy-start.2
  78.0 0.1 copy.52
  78.1 0.9 copy-done.2
  79.1 0.2 fusion.8
  79.3 39.4 %all-gather.7.cloned.1.call-done = bf16[1024,1024]{1,0:T(8,128)(2,1)} async-done(((bf16[64,1024]{1,0:T(8,128)(2,1)}), bf16[1024,1024]{1,0:T(8,128)(2,1)}) %all-gather.7.cloned.1.call-update) | async-done | bytes 2097168 | tf_op jit(solution)/shard_map/all_gather | solution.py:28
  118.7 5.3 gather_fusion
  124.0 168.9 %all-gather.5.cloned.1.call-done = bf16[4096,1024]{1,0:T(8,128)(2,1)} async-done(((bf16[256,1024]{1,0:T(8,128)(2,1)}), bf16[4096,1024]{1,0:T(8,128)(2,1)}) %all-gather.5.cloned.1.call-update) | async-done | bytes 8388624 | tf_op jit(solution)/shard_map/all_gather | solution.py:21
  292.9 0.0 copy-start.3
  292.9 5.0 fusion.7
  298.0 0.0 copy-done.3
  298.0 0.7 multiply_reduce_fusion
  298.7 0.1 rsqrt.20
  298.8 235.3 %all-gather.9.cloned.1.call-done = bf16[1024,3072]{1,0:T(8,128)(2,1)} async-done(((bf16[32,3072]{1,0:T(8,128)(2,1)}), bf16[1024,3072]{1,0:T(8,128)(2,1)}) %all-gather.9.cloned.1.call-update) | async-done | bytes 6291472 | tf_op jit(solution)/shard_map/all_gather | solution.py:42
  534.1 8.6 %convolution_convert_fusion = bf16[512,3072]{1,0:T(8,128)(2,1)} fusion(bf16[1024,3072]{1,0:T(8,128)(2,1)} %all-gather.9.cloned.1.call-done, f32[1024]{0:T(1024)S(1)} %convert_element_type.64, f32[512]{0:T(512)S(1)} %rsqrt.20, f32[64,1024]{1,0:T(8,128)S(1)} %fusion.7, bf16[512,1024]{1,0:T(8,128)(2,1)} %gather_fusion, ...), kind=kOutput, calls=%fused_computation.2 | convolution fusion | flops 3226468352 | bytes 10755072 | tf_op jit(solution)/shard_map/dot_general | solution.py:40
  542.7 8.6 %reshape.110 = bf16[64,8,3,16,64]{4,3,2,1,0:T(8,128)(2,1)} reshape(bf16[512,3072]{1,0:T(8,128)(2,1)} %convolution_convert_fusion) | data formatting | bytes 6291456 | tf_op jit(solution)/shard_map/reshape | solution.py:45
  551.3 6.9 %fusion.20 = (bf16[64,8,1,16,64]{4,3,2,1,0:T(8,128)(2,1)}, bf16[64,8,1,16,64]{4,3,2,1,0:T(8,128)(2,1)S(1)}, bf16[64,8,1,16,64]{4,3,2,1,0:T(8,128)(2,1)S(1)}) fusion(bf16[64,8,3,16,64]{4,3,2,1,0:T(8,128)(2,1)} %reshape.110), kind=kLoop, calls=%fused_computation.49 | loop fusion | bytes 6291456 | tf_op jit(solution)/shard_map/slice | solution.py:48
  558.2 3.3 fusion.1
  561.5 3.7 copy.46
  565.2 1.0 fusion.21
  566.3 0.1 divide_convert_fusion
  566.4 3.9 copy.47
  570.3 3.4 convert_bitcast_fusion
  573.7 2.0 copy.48
  575.7 0.0 copy-start.4
  575.7 4.2 reshape.111
  579.9 0.0 copy-done
  579.9 0.0 copy-done.4
  579.9 3.5 fusion.3
  (8 shorter events, 0.1 us)
Async XLA Ops:
  6.5 573.4 %copy-start = (bf16[1024,1024]{1,0:T(8,128)(2,1)S(1)}, bf16[1024,1024]{1,0:T(8,128)(2,1)}, u32[]{:S(2)}) copy-start(bf16[1024,1024]{1,0:T(8,128)(2,1)} %param.14) | copy-start | bytes 6291460
  6.5 70.3 %copy-start.5 = (s32[1,1,64,8]{2,3,1,0:T(8,128)S(1)}, s32[1,1,64,8]{2,3,1,0:T(8,128)}, u32[]{:S(2)}) copy-start(s32[1,1,64,8]{2,3,1,0:T(8,128)} %param.15) | copy-start | bytes 6148
  6.5 70.5 %copy-start.6 = (bf16[1024]{0:T(1024)(128)(2,1)S(1)}, bf16[1024]{0:T(1024)(128)(2,1)}, u32[]{:S(2)}) copy-start(bf16[1024]{0:T(1024)(128)(2,1)} %param.12) | copy-start | bytes 6148
  6.5 112.1 %all-gather.7.cloned.1.call-start = ((), (), s32[]{:S(2)}) async-start(), calls=%async_computation.2 | async-start | bytes 2228224 | tf_op jit(solution)/shard_map/all_gather | solution.py:28
  7.3 285.7 %all-gather.5.cloned.1.call-start = ((), (), s32[]{:S(2)}) async-start(), calls=%async_computation.1 | async-start | bytes 8912896 | tf_op jit(solution)/shard_map/all_gather | solution.py:21
  8.0 526.1 %all-gather.9.cloned.1.call-start = ((), (), s32[]{:S(2)}) async-start(), calls=%async_computation.3 | async-start | bytes 6488064 | tf_op jit(solution)/shard_map/all_gather | solution.py:42
  8.7 68.4 %all-to-all-start = ((bf16[16,64,256]{2,1,0:T(8,128)(2,1)}), bf16[16,64,256]{2,1,0:T(8,128)(2,1)S(1)}, u32[]{:S(2)}, u32[]{:S(2)}) async-start(bf16[16,64,256]{2,1,0:T(8,128)(2,1)} %bitcast.58), calls=%async_computation | async-start | bytes 1048576 | tf_op jit(solution)/shard_map/all_to_all | solution.py:18
  77.1 0.8 copy-start.1
  78.0 1.0 copy-start.2
  292.9 5.0 copy-start.3
  575.7 4.2 copy-start.4
Sparse Core Ops, SparseCore 0:
  10.6 108.0 all-gather.6
  122.0 170.9 all-gather.4
  295.0 239.0 all-gather.8
where the time goes:
time: 591 us; the launch traced here: 590 us
  waiting for transfers between devices  446 us (75%)
  blocking collectives  46 us (8%)
  local copies, waits for them, and re-layouts  38 us (6%)
  matrix products  23.9 us (4%)
  starting transfers between devices  18.2 us (3%)
  between operations  13.3 us (2%)
    all_gather x1, waiting for transfers between devices, per_device(): lax.all_gather(depth_proj, 'frame', axis=0, tiled=True)  235 us
    all_gather x1, waiting for transfers between devices, per_device(): rows_part = lax.all_gather(input_proj, 'fsdp', axis=0, tiled=True)  169 us
    all_gather x1, blocking collectives, per_device(): gain_part = lax.all_gather(norm_gain, 'fsdp', axis=0, tiled=True)  46 us
    all_gather x1, waiting for transfers between devices, per_device(): piece = lax.all_gather(code_table, 'fsdp', axis=0, tiled=True)  39.4 us
    all_to_all x1, starting transfers between devices, per_device(): lax.all_to_all(temporal_out, 'fsdp', split_axis=0, concat_axis=1, tiled=T...  18.1 us
  transfers between devices with their start and end apart: 4, of which 3 were waited for; matrix products, arithmetic and copies ran while one was open for 3% of the time, Pallas kernels for 0%

commit v1 on v0

v1 whole, which is shorter than its diff:
```python
import functools

import jax
import jax.numpy as jnp
from jax import lax
from jax.experimental import pallas as pl
from jax.experimental.pallas import tpu as pltpu
from jax.sharding import PartitionSpec as P

BF = jnp.bfloat16
F32 = jnp.float32
MESH = pl.DeviceIdType.MESH
NT = (((1,), (1,)), ((), ()))
N_REMOTE = 112


def dot(a, b):
    return jnp.dot(a, b, preferred_element_type=F32)


def kernel(
    temporal, gain, proj, table, dgain, dproj, dout, codes,
    out,
    tbuf, pbuf, gbuf, pacc, part, rel, rx, stg, zs, zr, zf,
    ssp, ssr, ssx, ssz,
    tab, emb, normed, stream,
    wb, qkv, mixed, doutb, outb,
    ssem, rsem, lsem,
):
    fs = lax.axis_index("fsdp")
    fr = lax.axis_index("frame")
    x, zh, c = fs // 4, lax.rem(fs // 2, 2), lax.rem(fs, 2)
    y, zl = fr // 8, lax.rem(fr, 8)
    z = zh * 8 + zl
    sib = 1 - c

    def at(dx=0, dy=0, dz=0, core=None):
        tx, ty, tz = lax.rem(x + dx + 4, 4), lax.rem(y + dy + 4, 4), lax.rem(z + dz + 16, 16)
        tc = c if core is None else core
        return (tx * 4 + (tz // 8) * 2 + tc, ty * 8 + lax.rem(tz, 8))

    x1, x2, x3 = lax.rem(x + 1, 4), lax.rem(x + 2, 4), lax.rem(x + 3, 4)
    y1, y2, y3 = lax.rem(y + 1, 4), lax.rem(y + 2, 4), lax.rem(y + 3, 4)

    started = []

    def send(src, dst, dev):
        index = len(started)
        copy = pltpu.make_async_remote_copy(
            src_ref=src, dst_ref=dst, send_sem=ssem.at[index], recv_sem=rsem.at[index],
            device_id=dev, device_id_type=MESH,
        )
        copy.start()
        started.append(copy)
        return copy

    locals_ = []

    def load(src, dst):
        copy = pltpu.make_async_copy(src, dst, lsem.at[len(locals_)])
        copy.start()
        locals_.append(copy)
        return copy

    j = x * 2 + c
    w_mine = pl.ds(pl.multiple_of(fr * 32, 32), 32)
    l_w = [
        load(
            dproj.at[:, pl.ds(pl.multiple_of(part_ * 1024 + j * 128, 128), 128)],
            wb.at[j, w_mine, pl.ds(part_ * 128, 128)],
        )
        for part_ in range(3)
    ]
    l_t = load(temporal.at[:, :, c], tbuf.at[c])
    l_p = load(proj, pbuf.at[c])
    l_tab = load(table, tab.at[fs])
    l_out = load(dout, doutb)
    gbuf[c] = jnp.broadcast_to(gain[...].astype(F32), (8, 256))

    partners = [at(core=sib), at(dx=1), at(dx=-1), at(dx=2), at(dy=1), at(dy=-1), at(dz=8)]
    partners += [at(dz=k) for k in (1, -1, 2, -2, 3, -3, 4, -4)]
    barrier = pltpu.get_barrier_semaphore()
    for partner in partners:
        pl.semaphore_signal(barrier, inc=1, device_id=partner, device_id_type=MESH)
    pl.semaphore_wait(barrier, len(partners))

    s_t = send(temporal.at[:, :, sib], tbuf.at[c], at(core=sib))
    s_p = send(proj, pbuf.at[c], at(core=sib))
    s_g = send(gbuf.at[c], gbuf.at[c], at(core=sib))
    for copy in l_w:
        copy.wait()
    s_wz = [
        send(wb.at[j, w_mine], wb.at[j, w_mine], at(dz=k)) for k in (4, 3, -3, 2, -2, 1, -1)
    ]
    quarter = pl.ds(pl.multiple_of(y * 16, 16), 16)
    s_tz = send(table.at[quarter], tab.at[fs, quarter], at(dz=8))
    s_tp = send(table, tab.at[fs], at(dx=1))
    s_tm = send(table, tab.at[fs], at(dx=-1))
    s_ts = send(table, tab.at[fs], at(core=sib))

    l_t.wait()
    l_p.wait()

    def scaled(k, half):
        rows = tbuf[k, :, half].reshape(256, 256).astype(F32)
        return (rows * gbuf[k][0:1]).astype(BF)

    far, near = 1 - zh, zh
    for side, half in ((0, far), (1, near)):
        pacc[side] = dot(scaled(c, half), pbuf[c])

    ids = codes[...]
    row = lax.broadcasted_iota(jnp.int32, (512, 64), 0)
    col = lax.broadcasted_iota(jnp.int32, (512, 64), 1)
    spread = (row // 8 == col).astype(BF)
    high = dot(spread, (ids // 32).astype(F32).astype(BF))
    low = dot(spread, lax.rem(ids, 32).astype(F32).astype(BF))
    row8 = lax.broadcasted_iota(jnp.int32, (512, 8), 0)
    col8 = lax.broadcasted_iota(jnp.int32, (512, 8), 1)
    picked = jnp.where(lax.rem(row8, 8) == col8, high * 32.0 + low, 0.0)
    id_col = jnp.sum(picked, axis=1, keepdims=True).astype(jnp.int32)

    s_t.wait_recv()
    s_p.wait_recv()
    s_g.wait_recv()
    s_x = []
    for side, half in ((0, far), (1, near)):
        total = pacc[side] + dot(scaled(sib, half), pbuf[sib])
        part[side] = total.astype(BF).reshape(4, 64, 1024)
        s_x.append((
            send(part.at[side, x2, 0:32], rel.at[side, 0], at(dx=1)),
            send(part.at[side, x2, 32:64], rel.at[side, 1], at(dx=-1)),
            send(part.at[side, x1, 32:64], rx.at[side, 0, 32:64], at(dx=1)),
            send(part.at[side, x3, 0:32], rx.at[side, 1, 0:32], at(dx=-1)),
        ))

    ones = jnp.ones((8, 256), BF)
    squares = jnp.zeros((8, 512), F32)
    for k in range(2):
        rows = tbuf[k].reshape(512, 256).astype(F32)
        sq = rows * rows
        hi = sq.astype(BF)
        lo = (sq - hi.astype(F32)).astype(BF)
        squares += lax.dot_general(ones, hi, NT, preferred_element_type=F32)
        squares += lax.dot_general(ones, lo, NT, preferred_element_type=F32)
    for k in range(4):
        ssp[k] = squares[:, 128 * k : 128 * (k + 1)]
    s_ss = [
        send(ssp.at[x1], ssr.at[0], at(dx=1)),
        send(ssp.at[x3], ssr.at[1], at(dx=-1)),
        send(ssp.at[x2], ssr.at[2], at(dx=2)),
    ]

    pieces = [lax.rem(x + k, 4) * 2 + c for k in (0, 3, 1, 2)]
    sib_pieces = [lax.rem(x + k, 4) * 2 + sib for k in (0, 3, 1, 2)]

    def block(yy):
        return pl.ds(pl.multiple_of(yy * 256, 256), 256)

    def half_block(yy, k):
        return pl.ds(pl.multiple_of(yy * 256 + 128 * k, 128), 128)

    s_wy, s_ws = {}, {}

    def spread_piece(r):
        p = pieces[r]
        s_wy[r] = [
            send(wb.at[p, block(y)], wb.at[p, block(y)], at(dy=1)),
            send(wb.at[p, block(y)], wb.at[p, block(y)], at(dy=-1)),
        ]
        s_ws[r] = [send(wb.at[p, block(y)], wb.at[p, block(y)], at(core=sib))]

    def relay_piece(r):
        p = pieces[r]
        s_wy[r][0].wait_recv()
        s_wy[r].append(send(wb.at[p, half_block(y3, 0)], wb.at[p, half_block(y3, 0)], at(dy=1)))
        s_ws[r].append(send(wb.at[p, block(y3)], wb.at[p, block(y3)], at(core=sib)))
        s_wy[r][1].wait_recv()
        s_wy[r].append(send(wb.at[p, half_block(y1, 1)], wb.at[p, half_block(y1, 1)], at(dy=-1)))
        s_ws[r].append(send(wb.at[p, block(y1)], wb.at[p, block(y1)], at(core=sib)))

    def finish_piece(r):
        p = pieces[r]
        s_wy[r][2].wait_recv()
        s_wy[r][3].wait_recv()
        s_ws[r].append(send(wb.at[p, block(y2)], wb.at[p, block(y2)], at(core=sib)))

    for copy in s_wz:
        copy.wait_recv()
    s_wx = [
        send(wb.at[j, block(y)], wb.at[j, block(y)], at(dx=1)),
        send(wb.at[j, block(y)], wb.at[j, block(y)], at(dx=-1)),
    ]
    spread_piece(0)

    def second_hop(side):
        s_x[side][0].wait_recv()
        stg[side, 0] = (part[side, x1, 0:32].astype(F32) + rel[side, 0].astype(F32)).astype(BF)
        a = send(stg.at[side, 0], rx.at[side, 0, 0:32], at(dx=1))
        s_x[side][1].wait_recv()
        stg[side, 1] = (part[side, x3, 32:64].astype(F32) + rel[side, 1].astype(F32)).astype(BF)
        b = send(stg.at[side, 1], rx.at[side, 1, 32:64], at(dx=-1))
        return a, b

    def x_total(side, hops):
        for copy in s_x[side][2:] + hops:
            copy.wait_recv()
        total = part[side, x].astype(F32) + rx[side, 0].astype(F32)
        return total + rx[side, 1].astype(F32)

    hops_far = second_hop(0)
    fz = x * 4 + (1 - zh) * 2 + c
    s_tz.wait_recv()
    s_ty = [
        send(tab.at[fz, quarter], tab.at[fz, quarter], at(dy=1)),
        send(tab.at[fz, quarter], tab.at[fz, quarter], at(dy=-1)),
    ]
    hops_near = second_hop(1)

    zs[...] = x_total(0, hops_far).astype(BF)
    s_z = [
        send(zs.at[0:32], zr.at[0], at(dz=4)),
        send(zs.at[32:64], zr.at[1], at(dz=-4)),
    ]
    for copy in s_ss:
        copy.wait_recv()
    ssx[...] = ssp[x] + ssr[0] + ssr[1] + ssr[2]
    s_ssz = send(ssx, ssz, at(dz=8))

    s_ty[0].wait_recv()
    q3 = pl.ds(pl.multiple_of(y3 * 16, 16), 16)
    s_ty.append(send(tab.at[fz, q3], tab.at[fz, q3], at(dy=1)))
    s_ty[1].wait_recv()

    def relay_x():
        p = pieces[1]
        s_wx[0].wait_recv()
        s_wx.append(send(wb.at[p, half_block(y, 0)], wb.at[p, half_block(y, 0)], at(dx=1)))
        spread_piece(1)
        p = pieces[2]
        s_wx[1].wait_recv()
        s_wx.append(send(wb.at[p, half_block(y, 1)], wb.at[p, half_block(y, 1)], at(dx=-1)))
        spread_piece(2)

    relay_x()
    f3, f1 = x3 * 4 + zh * 2 + c, x1 * 4 + zh * 2 + c
    s_tp.wait_recv()
    s_tm.wait_recv()
    s_tx = [
        send(tab.at[f3, 0:32], tab.at[f3, 0:32], at(dx=1)),
        send(tab.at[f1, 32:64], tab.at[f1, 32:64], at(dx=-1)),
        send(tab.at[f3], tab.at[f3], at(core=sib)),
        send(tab.at[f1], tab.at[f1], at(core=sib)),
    ]
    s_ty[2].wait_recv()
    s_uz = [
        send(tab.at[fz], tab.at[fz], at(dx=1)),
        send(tab.at[fz], tab.at[fz], at(dx=-1)),
        send(tab.at[fz], tab.at[fz], at(core=sib)),
    ]
    relay_piece(0)

    s_z[0].wait_recv()
    s_zz = [send(zr.at[0], zf.at[0:32], at(dz=4))]
    s_z[1].wait_recv()
    s_zz.append(send(zr.at[1], zf.at[32:64], at(dz=-4)))

    s_wx[2].wait_recv()
    s_wx[3].wait_recv()
    spread_piece(3)
    finish_piece(0)

    f2 = x2 * 4 + zh * 2 + c
    s_tx[0].wait_recv()
    s_tx[1].wait_recv()
    s_tx.append(send(tab.at[f2], tab.at[f2], at(core=sib)))
    g3, g1 = x3 * 4 + (1 - zh) * 2 + c, x1 * 4 + (1 - zh) * 2 + c
    s_uz[0].wait_recv()
    s_uz[1].wait_recv()
    s_ux = [
        send(tab.at[g3, 0:32], tab.at[g3, 0:32], at(dx=1)),
        send(tab.at[g1, 32:64], tab.at[g1, 32:64], at(dx=-1)),
        send(tab.at[g3], tab.at[g3], at(core=sib)),
        send(tab.at[g1], tab.at[g1], at(core=sib)),
    ]
    relay_piece(1)
    s_ux[0].wait_recv()
    s_ux[1].wait_recv()
    g2 = x2 * 4 + (1 - zh) * 2 + c
    s_ux.append(send(tab.at[g2], tab.at[g2], at(core=sib)))
    l_tab.wait()
    for copy in [s_ts, s_tx[2], s_tx[3], s_tx[4], s_uz[2], s_ux[2], s_ux[3], s_ux[4]]:
        copy.wait_recv()

    lanes = lax.broadcasted_iota(jnp.int32, (128, 1024), 1)
    whole_table = tab[...].reshape(1024, 1024)
    for t in range(4):
        onehot = (lanes == id_col[128 * t : 128 * (t + 1)]).astype(F32).astype(BF)
        emb[128 * t : 128 * (t + 1)] = dot(onehot, whole_table).astype(BF)
    finish_piece(1)
    relay_piece(2)

    near_total = x_total(1, hops_near)
    s_ssz.wait_recv()
    sums = ssx[...] + ssz[...]
    for copy in s_zz:
        copy.wait_recv()
    lane = lax.broadcasted_iota(jnp.int32, (64, 128), 1)
    sub = lax.broadcasted_iota(jnp.int32, (64, 128), 0)
    sum_col = jnp.sum(
        jnp.where(lane == sub + 64 * zh, sums[0:1], 0.0), axis=1, keepdims=True
    )
    inv_rms = lax.rsqrt(sum_col * (1.0 / 4096.0) + 1e-05)
    context = ((near_total + zf[...].astype(F32)) * inv_rms).astype(BF).astype(F32)
    depth_gain = dgain[...].astype(F32)
    for t in range(4):
        rows = slice(128 * t, 128 * (t + 1))
        wide = jnp.broadcast_to(context[16 * t : 16 * (t + 1)][:, None, :], (16, 8, 1024))
        value = wide.reshape(128, 1024) + emb[rows].astype(F32)
        inv = lax.rsqrt(jnp.mean(value * value, axis=-1, keepdims=True) + 1e-05)
        stream[rows] = value
        normed[rows] = (value * inv * depth_gain).astype(BF)
    finish_piece(2)
    relay_piece(3)

    first = lax.broadcasted_iota(jnp.int32, (128, 128), 1) < 64
    tr = lax.broadcasted_iota(jnp.int32, (128, 128), 0)
    tc = lax.broadcasted_iota(jnp.int32, (128, 128), 1)
    allowed = (tr // 8 == tc // 8) & (tc <= tr)

    def attend(p, slot):
        qkv[...] = dot(normed[...], wb[p]).astype(BF)

        def tile(t, carry):
            rows = pl.ds(pl.multiple_of(t * 128, 128), 128)
            q = qkv[rows, 0:128].astype(F32) * 0.125
            k = qkv[rows, 128:256]
            v = qkv[rows, 256:384]
            results = []
            for head in range(2):
                keep = first if head == 0 else jnp.logical_not(first)
                qh = jnp.where(keep, q, 0.0).astype(BF)
                scores = lax.dot_general(qh, k, NT, preferred_element_type=F32)
                scores = jnp.where(allowed, scores, -1e30)
                top = jnp.max(scores, axis=1, keepdims=True)
                e = jnp.exp(scores - top)
                weights = (e / jnp.sum(e, axis=1, keepdims=True)).astype(BF)
                results.append(dot(weights, v))
            mixed[rows, pl.ds(pl.multiple_of(slot * 128, 128), 128)] = jnp.where(
                first, results[0], results[1]
            ).astype(BF)
            return carry

        lax.fori_loop(0, 4, tile, 0)

    for r in range(4):
        if r == 3:
            finish_piece(3)
        attend(pieces[r], c)
        for copy in s_ws[r]:
            copy.wait_recv()
        attend(sib_pieces[r], sib)
        if r == 0:
            l_out.wait()
        weights_out = doutb[
            pl.ds(pl.multiple_of(lax.rem(x + (0, 3, 1, 2)[r], 4) * 256, 256), 256)
        ]
        if r < 3:
            stream[...] = stream[...] + dot(mixed[...], weights_out)
        else:
            stores = []
            for t in range(4):
                rows = slice(128 * t, 128 * (t + 1))
                outb[rows] = (stream[rows] + dot(mixed[rows], weights_out)).astype(BF)
                stores.append(load(outb.at[rows], out.at[rows]))
            for copy in stores:
                copy.wait()

    for copy in started:
        copy.wait_send()


def per_device(
    temporal_out, norm_gain, input_proj, code_table, depth_gain, depth_proj, depth_out, code_ids
):
    vmem = pl.BlockSpec(memory_space=pltpu.VMEM)
    hbm = pl.BlockSpec(memory_space=pl.ANY)
    scratch = [
        ((2, 4, 2, 64, 256), BF),
        ((2, 256, 1024), BF),
        ((2, 8, 256), F32),
        ((2, 256, 1024), F32),
        ((2, 4, 64, 1024), BF),
        ((2, 2, 32, 1024), BF),
        ((2, 2, 64, 1024), BF),
        ((2, 2, 32, 1024), BF),
        ((64, 1024), BF),
        ((2, 32, 1024), BF),
        ((64, 1024), BF),
        ((4, 8, 128), F32),
        ((3, 8, 128), F32),
        ((8, 128), F32),
        ((8, 128), F32),
        ((16, 64, 1024), BF),
        ((512, 1024), BF),
        ((512, 1024), BF),
        ((512, 1024), F32),
        ((8, 1024, 384), BF),
        ((512, 384), BF),
        ((512, 256), BF),
        ((1024, 1024), BF),
        ((512, 1024), BF),
    ]
    result = pl.pallas_call(
        kernel,
        out_shape=jax.ShapeDtypeStruct((512, 1024), BF),
        in_specs=[hbm, vmem, hbm, hbm, vmem, hbm, hbm, vmem],
        out_specs=hbm,
        scratch_shapes=[pltpu.VMEM(shape, dtype) for shape, dtype in scratch]
        + [
            pltpu.SemaphoreType.DMA((N_REMOTE,)),
            pltpu.SemaphoreType.DMA((N_REMOTE,)),
            pltpu.SemaphoreType.DMA((16,)),
        ],
        compiler_params=pltpu.CompilerParams(
            collective_id=0, has_side_effects=True, vmem_limit_bytes=56 * 1024 * 1024
        ),
        cost_estimate=pl.CostEstimate(
            flops=6_500_000_000, bytes_accessed=6_000_000, transcendentals=2_000_000
        ),
    )(
        temporal_out.reshape(4, 2, 2, 64, 256),
        norm_gain.reshape(1, 256),
        input_proj,
        code_table,
        depth_gain.reshape(1, 1024),
        depth_proj,
        depth_out,
        code_ids.reshape(64, 8),
    )
    return result.reshape(1, 1, 64, 8, 1024)


def solution(mesh):
    placed = (
        P("frame", "fsdp"),
        P("fsdp"),
        P("fsdp", None),
        P("fsdp", None),
        P(),
        P("frame", None),
        P(),
        P("frame", "fsdp", None, None),
    )
    return jax.shard_map(
        per_device,
        mesh=mesh,
        in_specs=placed,
        out_specs=P("frame", "fsdp", None, None, None),
        check_vma=False,
    )
```

time: 591 us -> 100 us (0.17)
  the two profiles are of different devices: /device:TPU:4 before, /device:TPU:1 now
where the time goes in v1:
time: 100 us
  Pallas kernels  93.9 us (94%)
  local copies, waits for them, and re-layouts  6.17 us (6%)
    pallas_call x1, Pallas kernels, per_device(): pl.pallas_call(kernel, out_shape=jax.ShapeDtypeStruct((512, 1024), BF), i...  93.9 us
    unnamed x2, local copies, waits for them, and re-layouts  3.65 us

profile of v1, /device:TPU:1, one launch (start us, length us, event | category | flops | bytes accessed | tf_op | source)
XLA Modules:
  0.0 100.1 jit_solution(6318965976611865672)
XLA Ops:
  0.0 1.2 %reshape.16.gain = bf16[1,256]{1,0:T(2,128)(2,1)} reshape(bf16[256]{0:T(256)(128)(2,1)} %param.9) | data formatting | bytes 1024 | tf_op jit(solution)/shard_map/reshape | solution.py:433
  1.2 1.3 %reshape.17.dgain = bf16[1,1024]{1,0:T(2,128)(2,1)} reshape(bf16[1024]{0:T(1024)(128)(2,1)} %param.12) | data formatting | bytes 4096 | tf_op jit(solution)/shard_map/reshape | solution.py:436
  2.5 1.4 %copy.9 = s32[1,1,64,8]{3,2,1,0:T(8,128)} copy(s32[1,1,64,8]{2,3,1,0:T(8,128)} %param.15) | data formatting | bytes 4096 | tf_op args[7]
  3.9 93.9 %shard_map.82 = bf16[512,1024]{1,0:T(8,128)(2,1)} custom-call(bf16[4,2,2,64,256]{4,3,2,1,0:T(8,128)(2,1)} %bitcast.5, bf16[1,256]{1,0:T(2,128)(2,1)} %reshape.16.gain, bf16[256,1024]{1,0:T(8,128)(2,1)} %proj.1, bf16[64,1024]{1,0:T(8,128)(2,1)} %table.1, bf16[1,1024]{1,0:T(2,128)(2,1)} %reshape.17.dgain, bf16[32,3072]{1,0:T(8,128)(2,1)} %dproj.1, ...), custom_call_target="tpu_custom_call" | custom-call | flops 6499999744 | bytes 6000000 | tf_op jit(solution)/shard_map/pallas_call | solution.py:414
  97.8 2.3 %copy.11 = bf16[1,1,64,8,1024]{4,3,2,1,0:T(8,128)(2,1)} copy(bf16[1,1,64,8,1024]{4,3,2,1,0:T(8,128)(2,1)} %bitcast.3) | data formatting | bytes 2097152

commit v2 on v1

v2 whole, which is shorter than its diff:
```python
import functools

import jax
import jax.numpy as jnp
from jax import lax
from jax.experimental import pallas as pl
from jax.experimental.pallas import tpu as pltpu
from jax.sharding import PartitionSpec as P

BF = jnp.bfloat16
F32 = jnp.float32
MESH = pl.DeviceIdType.MESH
NT = (((1,), (1,)), ((), ()))
N_REMOTE = 128


def dot(a, b):
    return jnp.dot(a, b, preferred_element_type=F32)


def kernel(
    temporal, gain, proj, table, dgain, dproj, dout, codes,
    out,
    tbuf, pbuf, gbuf, pacc, part, rel, rx, stg, fx, zs, zf,
    ssp, ssr, ssx, ssz,
    tab, emb, normed, stream,
    wb, qkv, comp, expand, mixed, doutb, outb,
    ssem, rsem, lsem,
):
    fs = lax.axis_index("fsdp")
    fr = lax.axis_index("frame")
    x, zh, c = fs // 4, lax.rem(fs // 2, 2), lax.rem(fs, 2)
    y, zl = fr // 8, lax.rem(fr, 8)
    z = zh * 8 + zl
    sib = 1 - c

    def at(dx=0, dy=0, dz=0, core=None):
        tx, ty, tz = lax.rem(x + dx + 4, 4), lax.rem(y + dy + 4, 4), lax.rem(z + dz + 16, 16)
        tc = c if core is None else core
        return (tx * 4 + (tz // 8) * 2 + tc, ty * 8 + lax.rem(tz, 8))

    x1, x2, x3 = lax.rem(x + 1, 4), lax.rem(x + 2, 4), lax.rem(x + 3, 4)
    y1, y2, y3 = lax.rem(y + 1, 4), lax.rem(y + 2, 4), lax.rem(y + 3, 4)

    started = []

    def send(src, dst, dev):
        index = len(started)
        copy = pltpu.make_async_remote_copy(
            src_ref=src, dst_ref=dst, send_sem=ssem.at[index], recv_sem=rsem.at[index],
            device_id=dev, device_id_type=MESH,
        )
        copy.start()
        started.append(copy)
        return copy

    locals_ = []

    def load(src, dst):
        copy = pltpu.make_async_copy(src, dst, lsem.at[len(locals_)])
        copy.start()
        locals_.append(copy)
        return copy

    mine = pl.ds(pl.multiple_of(c * 384, 128), 384)
    ring = [lax.rem(x + k, 4) for k in (0, 3, 1, 2)]

    def near_rows(yy, place):
        return pl.ds(pl.multiple_of(yy * 256 + 32 * place, 32), 32)

    def far_rows(yy):
        return pl.ds(pl.multiple_of(yy * 256 + 64, 32), 160)

    def far_half(yy, k):
        return pl.ds(pl.multiple_of(yy * 256 + 64 + 80 * k, 16), 80)

    l_w = [
        load(
            dproj.at[:, pl.ds(pl.multiple_of(k * 1024 + (2 * xx + c) * 128, 128), 128)],
            wb.at[xx, near_rows(y, 0), pl.ds(pl.multiple_of(c * 384 + k * 128, 128), 128)],
        )
        for xx in range(4)
        for k in range(3)
    ]
    l_t = load(temporal.at[:, :, c], tbuf.at[c])
    l_p = load(proj, pbuf.at[c])
    l_tab = load(table, tab.at[fs])
    l_out = load(dout, doutb)
    gbuf[c] = jnp.broadcast_to(gain[...].astype(F32).reshape(1, 256), (8, 256))

    partners = [at(core=sib), at(dx=1), at(dx=-1), at(dx=2), at(dy=1), at(dy=-1), at(dy=2)]
    partners += [at(dz=k) for k in (1, -1, 2, -2, 3, -3, 4, -4, 8)]
    barrier = pltpu.get_barrier_semaphore()
    for partner in partners:
        pl.semaphore_signal(barrier, inc=1, device_id=partner, device_id_type=MESH)
    pl.semaphore_wait(barrier, len(partners))

    s_t = send(temporal.at[:, :, sib], tbuf.at[c], at(core=sib))
    s_p = send(proj, pbuf.at[c], at(core=sib))
    s_g = send(gbuf.at[c], gbuf.at[c], at(core=sib))
    for copy in l_w:
        copy.wait()

    def send_w(xx, rows, **to):
        ref = wb.at[xx, rows, mine]
        return send(ref, ref, at(**to))

    s_wz = [
        send(wb.at[x, near_rows(y, 0), mine], wb.at[x, near_rows(y, -k % 8), mine], at(dz=k))
        for k in (4, 3, -3, 2, -2)
    ]
    s_wn = [
        send(wb.at[:, near_rows(y, 0), mine], wb.at[:, near_rows(y, -k % 8), mine], at(dz=k))
        for k in (1, -1)
    ]
    every = slice(0, 4)
    up = {0: send_w(every, near_rows(y, 0), dy=1)}
    down = {0: send_w(every, near_rows(y, 0), dy=-1)}
    quarter = pl.ds(pl.multiple_of(y * 16, 16), 16)
    s_tz = send(table.at[quarter], tab.at[fs, quarter], at(dz=8))
    s_tp = send(table, tab.at[fs], at(dx=1))
    s_tm = send(table, tab.at[fs], at(dx=-1))
    s_ts = send(table, tab.at[fs], at(core=sib))

    l_t.wait()
    l_p.wait()

    def scaled(k, half):
        rows = tbuf[k, :, half].reshape(256, 256).astype(F32)
        return (rows * gbuf[k][0:1]).astype(BF)

    far, near = 1 - zh, zh
    for side, half in ((0, far), (1, near)):
        pacc[side] = dot(scaled(c, half), pbuf[c])
    s_t.wait_recv()
    s_p.wait_recv()
    s_g.wait_recv()

    def partial(side, half):
        total = pacc[side] + dot(scaled(sib, half), pbuf[sib])
        part[side] = total.astype(BF).reshape(4, 64, 1024)

    partial(0, far)
    s_f = []
    for k in range(2):
        rows = slice(32 * k, 32 * k + 32)
        s_f.append([
            send(part.at[0, x2, rows], fx.at[2, rows], at(dx=2)),
            send(part.at[0, x1, rows], fx.at[0, rows], at(dx=1)),
            send(part.at[0, x3, rows], fx.at[1, rows], at(dx=-1)),
        ])
    partial(1, near)

    def first_hop():
        return (
            send(part.at[1, x2, 0:32], rel.at[0], at(dx=1)),
            send(part.at[1, x2, 32:64], rel.at[1], at(dx=-1)),
            send(part.at[1, x1, 32:64], rx.at[0, 32:64], at(dx=1)),
            send(part.at[1, x3, 0:32], rx.at[1, 0:32], at(dx=-1)),
        )

    def second_hop():
        s_x[0].wait_recv()
        stg[0] = (part[1, x1, 0:32].astype(F32) + rel[0].astype(F32)).astype(BF)
        a = send(stg.at[0], rx.at[0, 0:32], at(dx=1))
        s_x[1].wait_recv()
        stg[1] = (part[1, x3, 32:64].astype(F32) + rel[1].astype(F32)).astype(BF)
        b = send(stg.at[1], rx.at[1, 32:64], at(dx=-1))
        return a, b

    def spread_near(place):
        up[place] = send_w(every, near_rows(y, place), dy=1)
        down[place] = send_w(every, near_rows(y, place), dy=-1)

    s_yn, s_sn = [], []

    def relay_near(place):
        up[place].wait_recv()
        s_yn.append(send_w(slice(0, 2), near_rows(y3, place), dy=1))
        down[place].wait_recv()
        s_yn.append(send_w(slice(2, 4), near_rows(y1, place), dy=-1))

    def share_near(yy):
        s_sn.append(send_w(every, pl.ds(pl.multiple_of(yy * 256, 256), 64), core=sib))
        s_sn.append(send_w(every, near_rows(yy, 7), core=sib))

    s_wn[0].wait_recv()
    spread_near(7)
    s_wn[1].wait_recv()
    spread_near(1)
    share_near(y)
    relay_near(0)

    s_wy, s_ws = {}, {}

    def spread_far(r):
        s_wy[r] = [send_w(ring[r], far_rows(y), dy=1), send_w(ring[r], far_rows(y), dy=-1)]
        s_ws[r] = [send_w(ring[r], far_rows(y), core=sib)]

    def relay_far(r):
        s_wy[r][0].wait_recv()
        s_wy[r].append(send_w(ring[r], far_half(y3, 0), dy=1))
        s_ws[r].append(send_w(ring[r], far_rows(y3), core=sib))
        s_wy[r][1].wait_recv()
        s_wy[r].append(send_w(ring[r], far_half(y1, 1), dy=-1))
        s_ws[r].append(send_w(ring[r], far_rows(y1), core=sib))

    def finish_far(r):
        for copy in s_wy[r][2:]:
            copy.wait_recv()
        s_ws[r].append(send_w(ring[r], far_rows(y2), core=sib))

    def across(k):
        rows = slice(32 * k, 32 * k + 32)
        for copy in s_f[k]:
            copy.wait_recv()
        total = part[0, x, rows].astype(F32) + fx[0, rows].astype(F32)
        total = total + fx[1, rows].astype(F32) + fx[2, rows].astype(F32)
        zs[rows] = total.astype(BF)
        return send(zs.at[rows], zf.at[rows], at(dz=8))

    s_z = [across(0)]
    for copy in s_wz:
        copy.wait_recv()
    s_wx = [send_w(x, far_rows(y), dx=1), send_w(x, far_rows(y), dx=-1)]
    spread_far(0)
    relay_near(7)
    relay_near(1)
    s_z.append(across(1))
    s_x = first_hop()

    ones = jnp.ones((8, 256), BF)
    squares = jnp.zeros((8, 512), F32)
    for k in range(2):
        rows = tbuf[k].reshape(512, 256).astype(F32)
        sq = rows * rows
        hi = sq.astype(BF)
        lo = (sq - hi.astype(F32)).astype(BF)
        squares += lax.dot_general(ones, hi, NT, preferred_element_type=F32)
        squares += lax.dot_general(ones, lo, NT, preferred_element_type=F32)
    for k in range(4):
        ssp[k] = squares[:, 128 * k : 128 * (k + 1)]
    s_ss = [
        send(ssp.at[x1], ssr.at[0], at(dx=1)),
        send(ssp.at[x3], ssr.at[1], at(dx=-1)),
        send(ssp.at[x2], ssr.at[2], at(dx=2)),
    ]

    ids = codes[...]
    row = lax.broadcasted_iota(jnp.int32, (512, 64), 0)
    col = lax.broadcasted_iota(jnp.int32, (512, 64), 1)
    spread = (row // 8 == col).astype(BF)
    high = (ids // 32).astype(F32).astype(BF)
    low = lax.rem(ids, 32).astype(F32).astype(BF)
    high = lax.dot_general(spread, high, NT, preferred_element_type=F32)
    low = lax.dot_general(spread, low, NT, preferred_element_type=F32)
    row8 = lax.broadcasted_iota(jnp.int32, (512, 8), 0)
    col8 = lax.broadcasted_iota(jnp.int32, (512, 8), 1)
    picked = jnp.where(lax.rem(row8, 8) == col8, high * 32.0 + low, 0.0)
    id_col = jnp.sum(picked, axis=1, keepdims=True).astype(jnp.int32)

    fz = x * 4 + (1 - zh) * 2 + c
    s_tz.wait_recv()
    s_ty = [send(tab.at[fz, quarter], tab.at[fz, quarter], at(dy=k)) for k in (1, -1, 2)]

    er = lax.broadcasted_iota(jnp.int32, (128, 256), 0)
    ec = lax.broadcasted_iota(jnp.int32, (128, 256), 1)
    for u in range(8):
        expand[u] = ((er // 8 == 2 * u + ec // 128) & (lax.rem(er, 8) == lax.rem(ec, 8))).astype(
            F32
        ).astype(BF)

    s_wx[0].wait_recv()
    s_wx.append(send_w(ring[1], far_half(y, 0), dx=1))
    spread_far(1)
    s_wx[1].wait_recv()
    s_wx.append(send_w(ring[2], far_half(y, 1), dx=-1))
    spread_far(2)
    relay_far(0)
    hops = second_hop()
    for copy in s_ss:
        copy.wait_recv()
    ssx[...] = ssp[x] + ssr[0] + ssr[1] + ssr[2]
    s_ssz = send(ssx, ssz, at(dz=8))

    f3, f1 = x3 * 4 + zh * 2 + c, x1 * 4 + zh * 2 + c
    s_tp.wait_recv()
    s_tm.wait_recv()
    s_tx = [
        send(tab.at[f3, 0:32], tab.at[f3, 0:32], at(dx=1)),
        send(tab.at[f1, 32:64], tab.at[f1, 32:64], at(dx=-1)),
        send(tab.at[f3], tab.at[f3], at(core=sib)),
        send(tab.at[f1], tab.at[f1], at(core=sib)),
    ]
    for copy in s_ty:
        copy.wait_recv()
    s_uz = [
        send(tab.at[fz], tab.at[fz], at(dx=1)),
        send(tab.at[fz], tab.at[fz], at(dx=-1)),
        send(tab.at[fz], tab.at[fz], at(core=sib)),
    ]
    s_wx[2].wait_recv()
    s_wx[3].wait_recv()
    spread_far(3)
    for copy in s_yn:
        copy.wait_recv()
    for yy in (y1, y2, y3):
        share_near(yy)
    finish_far(0)

    f2 = x2 * 4 + zh * 2 + c
    s_tx[0].wait_recv()
    s_tx[1].wait_recv()
    s_tx.append(send(tab.at[f2], tab.at[f2], at(core=sib)))
    g3, g1 = x3 * 4 + (1 - zh) * 2 + c, x1 * 4 + (1 - zh) * 2 + c
    s_uz[0].wait_recv()
    s_uz[1].wait_recv()
    s_ux = [
        send(tab.at[g3, 0:32], tab.at[g3, 0:32], at(dx=1)),
        send(tab.at[g1, 32:64], tab.at[g1, 32:64], at(dx=-1)),
        send(tab.at[g3], tab.at[g3], at(core=sib)),
        send(tab.at[g1], tab.at[g1], at(core=sib)),
    ]
    relay_far(1)
    s_ux[0].wait_recv()
    s_ux[1].wait_recv()
    g2 = x2 * 4 + (1 - zh) * 2 + c
    s_ux.append(send(tab.at[g2], tab.at[g2], at(core=sib)))
    l_tab.wait()
    for copy in [s_ts, s_tx[2], s_tx[3], s_tx[4], s_uz[2], s_ux[2], s_ux[3], s_ux[4]]:
        copy.wait_recv()

    lanes = lax.broadcasted_iota(jnp.int32, (128, 1024), 1)
    whole_table = tab[...].reshape(1024, 1024)
    for t in range(4):
        onehot = (lanes == id_col[128 * t : 128 * (t + 1)]).astype(F32).astype(BF)
        emb[128 * t : 128 * (t + 1)] = dot(onehot, whole_table).astype(BF)

    for copy in s_x[2:] + hops:
        copy.wait_recv()
    total = part[1, x].astype(F32) + rx[0].astype(F32) + rx[1].astype(F32)
    s_ssz.wait_recv()
    sums = ssx[...] + ssz[...]
    lane = lax.broadcasted_iota(jnp.int32, (64, 128), 1)
    sub = lax.broadcasted_iota(jnp.int32, (64, 128), 0)
    sum_col = jnp.sum(
        jnp.where(lane == sub + 64 * zh, sums[0:1], 0.0), axis=1, keepdims=True
    )
    inv_rms = lax.rsqrt(sum_col * (1.0 / 4096.0) + 1e-05)
    for copy in s_z:
        copy.wait_recv()
    context = ((total + zf[...].astype(F32)) * inv_rms).astype(BF).astype(F32)
    depth_gain = dgain[...].astype(F32).reshape(1, 1024)
    turn = lax.rem(256 - 32 * zl, 256)
    for t in range(4):
        rows = slice(128 * t, 128 * (t + 1))
        wide = jnp.broadcast_to(context[16 * t : 16 * (t + 1)][:, None, :], (16, 8, 1024))
        value = wide.reshape(128, 1024) + emb[rows].astype(F32)
        inv = lax.rsqrt(jnp.mean(value * value, axis=-1, keepdims=True) + 1e-05)
        stream[rows] = value
        value = value * inv * depth_gain
        for k in range(4):
            part_k = pltpu.roll(value[:, 256 * k : 256 * (k + 1)], turn, 1)
            normed[rows, 256 * k : 256 * (k + 1)] = part_k.astype(BF)
    relay_far(2)

    first = lax.broadcasted_iota(jnp.int32, (128, 128), 1) < 64
    frame_of_lane = lax.broadcasted_iota(jnp.int32, (8, 128), 1) // 8
    position = lax.broadcasted_iota(jnp.int32, (128, 128), 0)
    query = lax.broadcasted_iota(jnp.int32, (128, 128), 1)
    allowed = lax.rem(position, 8) <= lax.rem(query, 8)
    same_frame = (
        lax.broadcasted_iota(jnp.int32, (128, 256), 0) // 8
        == lax.rem(lax.broadcasted_iota(jnp.int32, (128, 256), 1), 128) // 8
    )

    def by_head(a):
        a = a.astype(F32)
        return jnp.concatenate(
            [jnp.where(first, a, 0.0).astype(BF), jnp.where(first, 0.0, a).astype(BF)], axis=0
        )

    def attend(xx):
        qkv[...] = dot(normed[...], wb[xx]).astype(BF)
        for t in range(4):
            rows = slice(128 * t, 128 * (t + 1))
            for b in range(2):
                q = qkv[rows, 384 * b : 384 * b + 128]
                k = by_head(qkv[rows, 384 * b + 128 : 384 * b + 256])
                scores = lax.dot_general(k, q, NT, preferred_element_type=F32)
                for h in range(2):
                    own = scores[128 * h : 128 * h + 8]
                    for f in range(1, 16):
                        own = jnp.where(
                            frame_of_lane == f, scores[128 * h + 8 * f : 128 * h + 8 * f + 8], own
                        )
                    unit = t * 4 + b * 2 + h
                    comp[8 * unit : 8 * unit + 8] = own
        scores = jnp.where(allowed, comp[...] * 0.125, -1e30).reshape(16, 8, 128)
        e = jnp.exp(scores - jnp.max(scores, axis=1, keepdims=True))
        weights = (e / jnp.sum(e, axis=1, keepdims=True)).reshape(128, 128)
        weights = weights.T.astype(BF)
        for t in range(4):
            rows = slice(128 * t, 128 * (t + 1))
            for b in range(2):
                wide = dot(weights, expand[t * 2 + b])
                wide = jnp.where(same_frame, wide, 0.0).astype(BF)
                v = by_head(qkv[rows, 384 * b + 256 : 384 * b + 384])
                mixed[rows, 128 * b : 128 * b + 128] = dot(wide, v).astype(BF)

    l_out.wait()
    for copy in s_sn:
        copy.wait_recv()
    for r in range(4):
        if r > 0:
            finish_far(r)
        if r == 1:
            relay_far(3)
        for copy in s_ws[r]:
            copy.wait_recv()
        attend(ring[r])
        weights_out = doutb[pl.ds(pl.multiple_of(ring[r] * 256, 256), 256)]
        if r < 3:
            stream[...] = stream[...] + dot(mixed[...], weights_out)
        else:
            stores = []
            for t in range(4):
                rows = slice(128 * t, 128 * (t + 1))
                outb[rows] = (stream[rows] + dot(mixed[rows], weights_out)).astype(BF)
                stores.append(load(outb.at[rows], out.at[rows]))
            for copy in stores:
                copy.wait()

    for copy in started:
        copy.wait_send()


def per_device(
    temporal_out, norm_gain, input_proj, code_table, depth_gain, depth_proj, depth_out, code_ids
):
    vmem = pl.BlockSpec(memory_space=pltpu.VMEM)
    hbm = pl.BlockSpec(memory_space=pl.ANY)
    scratch = [
        ((2, 4, 2, 64, 256), BF),
        ((2, 256, 1024), BF),
        ((2, 8, 256), F32),
        ((2, 256, 1024), F32),
        ((2, 4, 64, 1024), BF),
        ((2, 32, 1024), BF),
        ((2, 64, 1024), BF),
        ((2, 32, 1024), BF),
        ((3, 64, 1024), BF),
        ((64, 1024), BF),
        ((64, 1024), BF),
        ((4, 8, 128), F32),
        ((3, 8, 128), F32),
        ((8, 128), F32),
        ((8, 128), F32),
        ((16, 64, 1024), BF),
        ((512, 1024), BF),
        ((512, 1024), BF),
        ((512, 1024), F32),
        ((4, 1024, 768), BF),
        ((512, 768), BF),
        ((128, 128), F32),
        ((8, 128, 256), BF),
        ((512, 256), BF),
        ((1024, 1024), BF),
        ((512, 1024), BF),
    ]
    operands = (
        temporal_out.reshape(4, 2, 2, 64, 256),
        norm_gain,
        input_proj,
        code_table,
        depth_gain,
        depth_proj,
        depth_out,
        code_ids.reshape(64, 8).T,
    )
    result = pl.pallas_call(
        kernel,
        out_shape=jax.ShapeDtypeStruct((512, 1024), BF),
        in_specs=[hbm, vmem, hbm, hbm, vmem, hbm, hbm, vmem],
        out_specs=hbm,
        scratch_shapes=[pltpu.VMEM(shape, dtype) for shape, dtype in scratch]
        + [
            pltpu.SemaphoreType.DMA((N_REMOTE,)),
            pltpu.SemaphoreType.DMA((N_REMOTE,)),
            pltpu.SemaphoreType.DMA((24,)),
        ],
        compiler_params=pltpu.CompilerParams(
            collective_id=0, has_side_effects=True, vmem_limit_bytes=40 * 1024 * 1024
        ),
        cost_estimate=pl.CostEstimate(
            flops=6_500_000_000, bytes_accessed=6_000_000, transcendentals=2_000_000
        ),
    )(*(pltpu.with_memory_space_constraint(a, pltpu.HBM) for a in operands))
    return result.reshape(1, 1, 64, 8, 1024)


def solution(mesh):
    placed = (
        P("frame", "fsdp"),
        P("fsdp"),
        P("fsdp", None),
        P("fsdp", None),
        P(),
        P("frame", None),
        P(),
        P("frame", "fsdp", None, None),
    )
    return jax.shard_map(
        per_device,
        mesh=mesh,
        in_specs=placed,
        out_specs=P("frame", "fsdp", None, None, None),
        check_vma=False,
    )
```

time: 100 us -> 75 us (0.75)
  the two profiles are of different devices: /device:TPU:1 before, /device:TPU:64 now
where the time goes in v2:
time: 75 us; the launch traced here: 74.8 us
  Pallas kernels  73.9 us (99%)
  local copies, waits for them, and re-layouts  0.97 us (1%)
    pallas_call x1, Pallas kernels, per_device(): pl.pallas_call(kernel, out_shape=jax.ShapeDtypeStruct((512, 1024), BF), i...  73.9 us

profile of v2, /device:TPU:64, one launch (start us, length us, event | category | flops | bytes accessed | tf_op | source)
XLA Modules:
  0.0 74.8 jit_solution(757597033216377160)
XLA Ops:
  0.0 73.9 %shard_map.82 = bf16[512,1024]{1,0:T(8,128)(2,1)S(1)} custom-call(bf16[4,2,2,64,256]{4,3,2,1,0:T(8,128)(2,1)} %bitcast.6, bf16[256]{0:T(256)(128)(2,1)} %gain.1, bf16[256,1024]{1,0:T(8,128)(2,1)} %proj.1, bf16[64,1024]{1,0:T(8,128)(2,1)} %table.1, bf16[1024]{0:T(1024)(128)(2,1)} %dgain.1, bf16[32,3072]{1,0:T(8,128)(2,1)} %dproj.1, bf16[1024,1024]{1,0:T(8,128)(2,1)} %dout.1, ...), custom_call_target="tpu_custom_call" | custom-call | flops 6499999744 | bytes 6000000 | tf_op jit(solution)/shard_map/pallas_call | solution.py:481
  73.9 1.0 %copy.10 = bf16[1,1,64,8,1024]{4,3,2,1,0:T(8,128)(2,1)} copy(bf16[1,1,64,8,1024]{4,3,2,1,0:T(8,128)(2,1)S(1)} %bitcast.5) | data formatting | bytes 2097152

commit v3 on v2

v3 whole, which is shorter than its diff:
```python
import functools

import jax
import jax.numpy as jnp
from jax import lax
from jax.experimental import pallas as pl
from jax.experimental.pallas import tpu as pltpu
from jax.sharding import PartitionSpec as P

BF = jnp.bfloat16
F32 = jnp.float32
MESH = pl.DeviceIdType.MESH
NT = (((1,), (1,)), ((), ()))
TN = (((0,), (0,)), ((), ()))
N_REMOTE = 128


def dot(a, b):
    return jnp.dot(a, b, preferred_element_type=F32)


def kernel(
    temporal, gain, proj, table, dgain, dproj, dout, codes,
    out,
    tbuf, pbuf, gbuf, pacc, part, rel, rx, stg, fx, zs, zf,
    ssp, ssr, ssx, ssz,
    tab, emb, normed, stream,
    wb, qkv, comp, mixed, doutb, outb,
    ssem, rsem, lsem,
):
    fs = lax.axis_index("fsdp")
    fr = lax.axis_index("frame")
    x, zh, c = fs // 4, lax.rem(fs // 2, 2), lax.rem(fs, 2)
    y, zl = fr // 8, lax.rem(fr, 8)
    z = zh * 8 + zl
    sib = 1 - c

    def at(dx=0, dy=0, dz=0, core=None):
        tx, ty, tz = lax.rem(x + dx + 4, 4), lax.rem(y + dy + 4, 4), lax.rem(z + dz + 16, 16)
        tc = c if core is None else core
        return (tx * 4 + (tz // 8) * 2 + tc, ty * 8 + lax.rem(tz, 8))

    x1, x2, x3 = lax.rem(x + 1, 4), lax.rem(x + 2, 4), lax.rem(x + 3, 4)
    y1, y2, y3 = lax.rem(y + 1, 4), lax.rem(y + 2, 4), lax.rem(y + 3, 4)

    started = []

    def send(src, dst, dev):
        index = len(started)
        copy = pltpu.make_async_remote_copy(
            src_ref=src, dst_ref=dst, send_sem=ssem.at[index], recv_sem=rsem.at[index],
            device_id=dev, device_id_type=MESH,
        )
        copy.start()
        started.append(copy)
        return copy

    locals_ = []

    def load(src, dst):
        copy = pltpu.make_async_copy(src, dst, lsem.at[len(locals_)])
        copy.start()
        locals_.append(copy)
        return copy

    mine = pl.ds(pl.multiple_of(c * 384, 128), 384)
    ring = [lax.rem(x + k, 4) for k in range(4)]

    def at_place(yy, place):
        return pl.ds(pl.multiple_of(yy * 256 + 32 * place, 32), 32)

    def far_rows(yy):
        return pl.ds(pl.multiple_of(yy * 256 + 96, 32), 96)

    def far_half(yy, k):
        return pl.ds(pl.multiple_of(yy * 256 + 96 + 48 * k, 16), 48)

    l_w = [
        load(
            dproj.at[:, pl.ds(pl.multiple_of(k * 1024 + (2 * xx + c) * 128, 128), 128)],
            wb.at[xx, at_place(y, 0), pl.ds(pl.multiple_of(c * 384 + k * 128, 128), 128)],
        )
        for xx in range(4)
        for k in range(3)
    ]
    l_t = load(temporal.at[:, :, c], tbuf.at[c])
    l_p = load(proj, pbuf.at[c])
    l_tab = load(table, tab.at[fs])
    l_out = [
        load(dout.at[pl.ds(pl.multiple_of(ring[r] * 256, 256), 256)], doutb.at[256 * r : 256 * r + 256])
        for r in range(4)
    ]
    gbuf[c] = jnp.broadcast_to(gain[...].astype(F32).reshape(1, 256), (8, 256))

    partners = [at(core=sib)]
    partners += [at(dx=k) for k in (1, -1, 2)] + [at(dy=k) for k in (1, -1, 2)]
    partners += [at(dz=k) for k in (1, -1, 8)]
    barrier = pltpu.get_barrier_semaphore()
    for partner in partners:
        pl.semaphore_signal(barrier, inc=1, device_id=partner, device_id_type=MESH)
    pl.semaphore_wait(barrier, len(partners))

    quarter = pl.ds(pl.multiple_of(y * 16, 16), 16)
    s_tz = send(table.at[quarter], tab.at[fs, quarter], at(dz=8))
    for copy in l_w:
        copy.wait()

    def send_w(xx, rows, **to):
        ref = wb.at[xx, rows, mine]
        return send(ref, ref, at(**to))

    every = slice(0, 4)

    def along_z(place, dz, pieces=slice(0, 4)):
        return send(
            wb.at[pieces, at_place(y, place), mine],
            wb.at[pieces, at_place(y, (place - dz) % 8), mine],
            at(dz=dz),
        )

    halves = (slice(0, 2), slice(2, 4))
    from_z = {}
    for k in range(2):
        for place, dz in ((7, 1), (1, -1)):
            from_z[place, k] = along_z(0, dz, halves[k])
    up = {0: send_w(every, at_place(y, 0), dy=1)}
    down = {0: send_w(every, at_place(y, 0), dy=-1)}
    s_t = send(temporal.at[:, :, sib], tbuf.at[c], at(core=sib))
    s_p = send(proj, pbuf.at[c], at(core=sib))
    s_g = send(gbuf.at[c], gbuf.at[c], at(core=sib))
    s_tp = send(table, tab.at[fs], at(dx=1))
    s_tm = send(table, tab.at[fs], at(dx=-1))
    s_ts = send(table, tab.at[fs], at(core=sib))

    l_t.wait()
    l_p.wait()

    def scaled(k, half):
        rows = tbuf[k, :, half].reshape(256, 256).astype(F32)
        return (rows * gbuf[k][0:1]).astype(BF)

    far, near = 1 - zh, zh
    for side, half in ((0, far), (1, near)):
        pacc[side] = dot(scaled(c, half), pbuf[c])
    s_t.wait_recv()
    s_p.wait_recv()
    s_g.wait_recv()

    def partial(side, half):
        total = pacc[side] + dot(scaled(sib, half), pbuf[sib])
        part[side] = total.astype(BF).reshape(4, 64, 1024)

    partial(0, far)
    s_f = []
    for k in range(2):
        rows = slice(32 * k, 32 * k + 32)
        s_f.append([
            send(part.at[0, x2, rows], fx.at[2, rows], at(dx=2)),
            send(part.at[0, x1, rows], fx.at[0, rows], at(dx=1)),
            send(part.at[0, x3, rows], fx.at[1, rows], at(dx=-1)),
        ])
    ones = jnp.ones((8, 256), BF)
    squares = jnp.zeros((8, 512), F32)
    for k in range(2):
        rows = tbuf[k].reshape(512, 256).astype(F32)
        sq = rows * rows
        hi = sq.astype(BF)
        lo = (sq - hi.astype(F32)).astype(BF)
        squares += lax.dot_general(ones, hi, NT, preferred_element_type=F32)
        squares += lax.dot_general(ones, lo, NT, preferred_element_type=F32)
    for k in range(4):
        ssp[k] = squares[:, 128 * k : 128 * (k + 1)]
    s_ss = [
        send(ssp.at[x1], ssr.at[0], at(dx=1)),
        send(ssp.at[x3], ssr.at[1], at(dx=-1)),
        send(ssp.at[x2], ssr.at[2], at(dx=2)),
    ]

    partial(1, near)

    def first_hop():
        return (
            send(part.at[1, x2, 0:32], rel.at[0], at(dx=1)),
            send(part.at[1, x2, 32:64], rel.at[1], at(dx=-1)),
            send(part.at[1, x1, 32:64], rx.at[0, 32:64], at(dx=1)),
            send(part.at[1, x3, 0:32], rx.at[1, 0:32], at(dx=-1)),
        )

    def second_hop():
        s_x[0].wait_recv()
        stg[0] = (part[1, x1, 0:32].astype(F32) + rel[0].astype(F32)).astype(BF)
        a = send(stg.at[0], rx.at[0, 0:32], at(dx=1))
        s_x[1].wait_recv()
        stg[1] = (part[1, x3, 32:64].astype(F32) + rel[1].astype(F32)).astype(BF)
        b = send(stg.at[1], rx.at[1, 32:64], at(dx=-1))
        return a, b

    def spread_near(place):
        up[place] = send_w(every, at_place(y, place), dy=1)
        down[place] = send_w(every, at_place(y, place), dy=-1)

    s_yn, s_sn = [], []

    def relay_near(place):
        up[place].wait_recv()
        s_yn.append(send_w(slice(0, 2), at_place(y3, place), dy=1))
        down[place].wait_recv()
        s_yn.append(send_w(slice(2, 4), at_place(y1, place), dy=-1))

    def share_near(yy):
        for first_place, count in ((0, 3), (6, 2)):
            rows = pl.ds(pl.multiple_of(yy * 256 + 32 * first_place, 32), 32 * count)
            s_sn.append(send_w(every, rows, core=sib))

    s_wy, s_ws = {}, {}

    def spread_far(r):
        s_wy[r] = [send_w(ring[r], far_rows(y), dy=1), send_w(ring[r], far_rows(y), dy=-1)]
        s_ws[r] = [send_w(ring[r], far_rows(y), core=sib)]

    def relay_far(r):
        s_wy[r][0].wait_recv()
        s_wy[r].append(send_w(ring[r], far_half(y3, 0), dy=1))
        s_ws[r].append(send_w(ring[r], far_rows(y3), core=sib))
        s_wy[r][1].wait_recv()
        s_wy[r].append(send_w(ring[r], far_half(y1, 1), dy=-1))
        s_ws[r].append(send_w(ring[r], far_rows(y1), core=sib))

    def finish_far(r):
        for copy in s_wy[r][2:]:
            copy.wait_recv()
        s_ws[r].append(send_w(ring[r], far_rows(y2), core=sib))

    def across(k):
        rows = slice(32 * k, 32 * k + 32)
        for copy in s_f[k]:
            copy.wait_recv()
        total = part[0, x, rows].astype(F32) + fx[0, rows].astype(F32)
        total = total + fx[1, rows].astype(F32) + fx[2, rows].astype(F32)
        zs[rows] = total.astype(BF)
        return send(zs.at[rows], zf.at[rows], at(dz=8))

    def pass_on(up_place, down_place):
        for k in range(2):
            for place, dz in ((up_place, 1), (down_place, -1)):
                from_z[place, k].wait_recv()
                if place not in (3, 5) or (place == 5) == (k == 0):
                    from_z[(place - dz) % 8, k] = along_z(place, dz, halves[k])

    pass_on(7, 1)
    spread_near(7)
    relay_near(0)
    fz = x * 4 + (1 - zh) * 2 + c
    s_tz.wait_recv()
    s_ty = [send(tab.at[fz, quarter], tab.at[fz, quarter], at(dy=k)) for k in (1, -1, 2)]
    spread_near(1)
    f3, f1 = x3 * 4 + zh * 2 + c, x1 * 4 + zh * 2 + c
    s_tp.wait_recv()
    s_tm.wait_recv()
    s_tx = [
        send(tab.at[f3, 0:32], tab.at[f3, 0:32], at(dx=1)),
        send(tab.at[f1, 32:64], tab.at[f1, 32:64], at(dx=-1)),
        send(tab.at[f3], tab.at[f3], at(core=sib)),
        send(tab.at[f1], tab.at[f1], at(core=sib)),
    ]
    pass_on(6, 2)
    spread_near(6)
    s_z = [across(0), across(1)]
    spread_near(2)
    s_x = first_hop()
    for copy in s_ty:
        copy.wait_recv()
    s_uz = [send(tab.at[fz], tab.at[fz], at(dx=k)) for k in (2, 1, -1)]
    s_us = [send(tab.at[fz], tab.at[fz], at(core=sib))]
    share_near(y)
    pass_on(5, 3)
    relay_near(7)
    relay_near(1)
    hops = second_hop()

    ids = codes[...]
    row = lax.broadcasted_iota(jnp.int32, (512, 64), 0)
    col = lax.broadcasted_iota(jnp.int32, (512, 64), 1)
    spread = (row // 8 == col).astype(BF)
    high = (ids // 32).astype(F32).astype(BF)
    low = lax.rem(ids, 32).astype(F32).astype(BF)
    high = lax.dot_general(spread, high, NT, preferred_element_type=F32)
    low = lax.dot_general(spread, low, NT, preferred_element_type=F32)
    row8 = lax.broadcasted_iota(jnp.int32, (512, 8), 0)
    col8 = lax.broadcasted_iota(jnp.int32, (512, 8), 1)
    picked = jnp.where(lax.rem(row8, 8) == col8, high * 32.0 + low, 0.0)
    id_col = jnp.sum(picked, axis=1, keepdims=True).astype(jnp.int32)

    for copy in s_ss:
        copy.wait_recv()
    ssx[...] = ssp[x] + ssr[0] + ssr[1] + ssr[2]
    s_ssz = send(ssx, ssz, at(dz=8))
    f2 = x2 * 4 + zh * 2 + c
    s_tx[0].wait_recv()
    s_tx[1].wait_recv()
    s_tx.append(send(tab.at[f2], tab.at[f2], at(core=sib)))
    relay_near(6)
    relay_near(2)
    for copy, xx in zip(s_uz, (x2, x3, x1)):
        copy.wait_recv()
        ref = tab.at[xx * 4 + (1 - zh) * 2 + c]
        s_us.append(send(ref, ref, at(core=sib)))
    from_z[4, 0].wait_recv()
    from_z[4, 1].wait_recv()
    spread_far(0)
    spread_far(1)
    l_tab.wait()
    for copy in [s_ts] + s_tx[2:] + s_us:
        copy.wait_recv()

    lanes = lax.broadcasted_iota(jnp.int32, (128, 1024), 1)
    whole_table = tab[...].reshape(1024, 1024)
    for t in range(4):
        onehot = (lanes == id_col[128 * t : 128 * (t + 1)]).astype(F32).astype(BF)
        emb[128 * t : 128 * (t + 1)] = dot(onehot, whole_table).astype(BF)

    relay_far(0)
    spread_far(2)

    for copy in s_x[2:] + hops:
        copy.wait_recv()
    total = part[1, x].astype(F32) + rx[0].astype(F32) + rx[1].astype(F32)
    s_ssz.wait_recv()
    sums = ssx[...] + ssz[...]
    lane = lax.broadcasted_iota(jnp.int32, (64, 128), 1)
    sub = lax.broadcasted_iota(jnp.int32, (64, 128), 0)
    sum_col = jnp.sum(
        jnp.where(lane == sub + 64 * zh, sums[0:1], 0.0), axis=1, keepdims=True
    )
    inv_rms = lax.rsqrt(sum_col * (1.0 / 4096.0) + 1e-05)
    for copy in s_z:
        copy.wait_recv()
    context = ((total + zf[...].astype(F32)) * inv_rms).astype(BF).astype(F32)
    depth_gain = dgain[...].astype(F32).reshape(1, 1024)
    turn = lax.rem(256 - 32 * zl, 256)
    for t in range(4):
        rows = slice(128 * t, 128 * (t + 1))
        wide = jnp.broadcast_to(context[16 * t : 16 * (t + 1)][:, None, :], (16, 8, 1024))
        value = wide.reshape(128, 1024) + emb[rows].astype(F32)
        inv = lax.rsqrt(jnp.mean(value * value, axis=-1, keepdims=True) + 1e-05)
        stream[rows] = value
        value = value * inv * depth_gain
        for k in range(4):
            part_k = pltpu.roll(value[:, 256 * k : 256 * (k + 1)], turn, 1)
            normed[rows, 256 * k : 256 * (k + 1)] = part_k.astype(BF)
    relay_far(1)
    spread_far(3)
    for copy in s_yn:
        copy.wait_recv()
    for yy in (y1, y2, y3):
        share_near(yy)
    finish_far(0)
    relay_far(2)
    finish_far(1)

    first = lax.broadcasted_iota(jnp.int32, (128, 128), 1) < 64
    frame_of_lane = lax.broadcasted_iota(jnp.int32, (8, 128), 1) // 8
    position = lax.broadcasted_iota(jnp.int32, (128, 128), 0)
    query = lax.broadcasted_iota(jnp.int32, (128, 128), 1)
    allowed = lax.rem(position, 8) <= lax.rem(query, 8)
    def by_head(a):
        a = a.astype(F32)
        return jnp.concatenate(
            [jnp.where(first, a, 0.0).astype(BF), jnp.where(first, 0.0, a).astype(BF)], axis=0
        )

    def attend(r):
        for t in range(2):
            rows = slice(256 * t, 256 * (t + 1))
            qkv[rows] = dot(normed[rows], wb[ring[r]]).astype(BF)
        for t in range(4):
            rows = slice(128 * t, 128 * (t + 1))
            for b in range(2):
                q = qkv[rows, 384 * b : 384 * b + 128]
                k = by_head(qkv[rows, 384 * b + 128 : 384 * b + 256])
                scores = lax.dot_general(k, q, NT, preferred_element_type=F32)
                for h in range(2):
                    own = scores[128 * h : 128 * h + 8]
                    for f in range(1, 16):
                        own = jnp.where(
                            frame_of_lane == f, scores[128 * h + 8 * f : 128 * h + 8 * f + 8], own
                        )
                    unit = t * 4 + b * 2 + h
                    comp[8 * unit : 8 * unit + 8] = own
        scores = jnp.where(allowed, comp[...] * 0.125, -1e30).reshape(16, 8, 128)
        e = jnp.exp(scores - jnp.max(scores, axis=1, keepdims=True))
        weights = (e / jnp.sum(e, axis=1, keepdims=True)).reshape(128, 128)
        for t in range(4):
            rows = slice(128 * t, 128 * (t + 1))
            for b in range(2):
                wide = []
                for unit in (t * 4 + b * 2, t * 4 + b * 2 + 1):
                    own = weights[8 * unit : 8 * unit + 8]
                    wide += [jnp.where(frame_of_lane == f, own, 0.0) for f in range(16)]
                wide = jnp.concatenate(wide, axis=0).astype(BF)
                v = by_head(qkv[rows, 384 * b + 256 : 384 * b + 384])
                mixed[rows, 256 * r + 128 * b : 256 * r + 128 * b + 128] = lax.dot_general(
                    wide, v, TN, preferred_element_type=F32
                ).astype(BF)

    for copy in l_out:
        copy.wait()
    for copy in s_sn:
        copy.wait_recv()
    for r in range(4):
        if r == 1:
            finish_far(2)
            relay_far(3)
        if r == 2:
            finish_far(3)
        for copy in s_ws[r]:
            copy.wait_recv()
        attend(r)
    stores = []
    for t in range(4):
        rows = slice(128 * t, 128 * (t + 1))
        outb[rows] = (stream[rows] + dot(mixed[rows], doutb[...])).astype(BF)
        stores.append(load(outb.at[rows], out.at[rows]))
    for copy in stores:
        copy.wait()

    for copy in started:
        copy.wait_send()


def per_device(
    temporal_out, norm_gain, input_proj, code_table, depth_gain, depth_proj, depth_out, code_ids
):
    vmem = pl.BlockSpec(memory_space=pltpu.VMEM)
    hbm = pl.BlockSpec(memory_space=pl.ANY)
    scratch = [
        ((2, 4, 2, 64, 256), BF),
        ((2, 256, 1024), BF),
        ((2, 8, 256), F32),
        ((2, 256, 1024), F32),
        ((2, 4, 64, 1024), BF),
        ((2, 32, 1024), BF),
        ((2, 64, 1024), BF),
        ((2, 32, 1024), BF),
        ((3, 64, 1024), BF),
        ((64, 1024), BF),
        ((64, 1024), BF),
        ((4, 8, 128), F32),
        ((3, 8, 128), F32),
        ((8, 128), F32),
        ((8, 128), F32),
        ((16, 64, 1024), BF),
        ((512, 1024), BF),
        ((512, 1024), BF),
        ((512, 1024), F32),
        ((4, 1024, 768), BF),
        ((512, 768), BF),
        ((128, 128), F32),
        ((512, 1024), BF),
        ((1024, 1024), BF),
        ((512, 1024), BF),
    ]
    operands = (
        temporal_out.reshape(4, 2, 2, 64, 256),
        norm_gain,
        input_proj,
        code_table,
        depth_gain,
        depth_proj,
        depth_out,
        code_ids.reshape(64, 8).T,
    )
    result = pl.pallas_call(
        kernel,
        out_shape=jax.ShapeDtypeStruct((512, 1024), BF),
        in_specs=[hbm, vmem, hbm, hbm, vmem, hbm, hbm, vmem],
        out_specs=hbm,
        scratch_shapes=[pltpu.VMEM(shape, dtype) for shape, dtype in scratch]
        + [
            pltpu.SemaphoreType.DMA((N_REMOTE,)),
            pltpu.SemaphoreType.DMA((N_REMOTE,)),
            pltpu.SemaphoreType.DMA((32,)),
        ],
        compiler_params=pltpu.CompilerParams(
            collective_id=0, has_side_effects=True, vmem_limit_bytes=40 * 1024 * 1024
        ),
        cost_estimate=pl.CostEstimate(
            flops=6_500_000_000, bytes_accessed=6_000_000, transcendentals=2_000_000
        ),
    )(*(pltpu.with_memory_space_constraint(a, pltpu.HBM) for a in operands))
    return result.reshape(1, 1, 64, 8, 1024)


def solution(mesh):
    placed = (
        P("frame", "fsdp"),
        P("fsdp"),
        P("fsdp", None),
        P("fsdp", None),
        P(),
        P("frame", None),
        P(),
        P("frame", "fsdp", None, None),
    )
    return jax.shard_map(
        per_device,
        mesh=mesh,
        in_specs=placed,
        out_specs=P("frame", "fsdp", None, None, None),
        check_vma=False,
    )
```

time: 75 us -> 67.7 us (0.903)
  Pallas kernels: 73.9 us -> 66.6 us
    pallas_call x1, Pallas kernels: 73.9 us -> 66.6 us  [per_device(): pl.pallas_call(kernel, out_shape=jax.ShapeDtypeStruct((512, 1024), BF), i...]
where the time goes in v3:
time: 67.7 us; the launch traced here: 67.6 us
  Pallas kernels  66.6 us (98%)
  local copies, waits for them, and re-layouts  0.97 us (1%)
    pallas_call x1, Pallas kernels, per_device(): pl.pallas_call(kernel, out_shape=jax.ShapeDtypeStruct((512, 1024), BF), i...  66.6 us

profile of v3, /device:TPU:64, one launch (start us, length us, event | category | flops | bytes accessed | tf_op | source)
XLA Modules:
  0.0 67.6 jit_solution(6242010683557166980)
XLA Ops:
  0.0 66.6 %shard_map.82 = bf16[512,1024]{1,0:T(8,128)(2,1)S(1)} custom-call(bf16[4,2,2,64,256]{4,3,2,1,0:T(8,128)(2,1)} %bitcast.6, bf16[256]{0:T(256)(128)(2,1)} %gain.1, bf16[256,1024]{1,0:T(8,128)(2,1)} %proj.1, bf16[64,1024]{1,0:T(8,128)(2,1)} %table.1, bf16[1024]{0:T(1024)(128)(2,1)} %dgain.1, bf16[32,3072]{1,0:T(8,128)(2,1)} %dproj.1, bf16[1024,1024]{1,0:T(8,128)(2,1)} %dout.1, ...), custom_call_target="tpu_custom_call" | custom-call | flops 6499999744 | bytes 6000000 | tf_op jit(solution)/shard_map/pallas_call | solution.py:473
  66.6 1.0 %copy.10 = bf16[1,1,64,8,1024]{4,3,2,1,0:T(8,128)(2,1)} copy(bf16[1,1,64,8,1024]{4,3,2,1,0:T(8,128)(2,1)S(1)} %bitcast.5) | data formatting | bytes 2097152

commit v4 on v3

--- a/solution.py
+++ b/solution.py
@@ -64,16 +64,16 @@
         return copy
 
     mine = pl.ds(pl.multiple_of(c * 384, 128), 384)
-    ring = [lax.rem(x + k, 4) for k in range(4)]
+    ring = [lax.rem(x + k, 4) for k in (0, 3, 1, 2)]
 
     def at_place(yy, place):
         return pl.ds(pl.multiple_of(yy * 256 + 32 * place, 32), 32)
 
     def far_rows(yy):
-        return pl.ds(pl.multiple_of(yy * 256 + 96, 32), 96)
+        return at_place(yy, 4)
 
     def far_half(yy, k):
-        return pl.ds(pl.multiple_of(yy * 256 + 96 + 48 * k, 16), 48)
+        return pl.ds(pl.multiple_of(yy * 256 + 128 + 16 * k, 16), 16)
 
     l_w = [
         load(
@@ -94,14 +94,16 @@
 
     partners = [at(core=sib)]
     partners += [at(dx=k) for k in (1, -1, 2)] + [at(dy=k) for k in (1, -1, 2)]
-    partners += [at(dz=k) for k in (1, -1, 8)]
+    partners += [at(dz=k) for k in (1, -1, 4, -4, 8)]
     barrier = pltpu.get_barrier_semaphore()
+    partners.append((x * 4 + (1 - zh) * 2 + c, y * 8 + 7 - zl))
     for partner in partners:
         pl.semaphore_signal(barrier, inc=1, device_id=partner, device_id_type=MESH)
     pl.semaphore_wait(barrier, len(partners))
 
     quarter = pl.ds(pl.multiple_of(y * 16, 16), 16)
-    s_tz = send(table.at[quarter], tab.at[fs, quarter], at(dz=8))
+    mirror = (x * 4 + (1 - zh) * 2 + c, y * 8 + 7 - zl)
+    s_tz = send(table.at[quarter], tab.at[fs, quarter], mirror)
     for copy in l_w:
         copy.wait()
 
@@ -125,6 +127,10 @@
             from_z[place, k] = along_z(0, dz, halves[k])
     up = {0: send_w(every, at_place(y, 0), dy=1)}
     down = {0: send_w(every, at_place(y, 0), dy=-1)}
+    far_z = [
+        send(wb.at[x, at_place(y, 0), mine], wb.at[x, at_place(y, -k % 8), mine], at(dz=k))
+        for k in (4,)
+    ]
     s_t = send(temporal.at[:, :, sib], tbuf.at[c], at(core=sib))
     s_p = send(proj, pbuf.at[c], at(core=sib))
     s_g = send(gbuf.at[c], gbuf.at[c], at(core=sib))
@@ -208,7 +214,7 @@
         s_yn.append(send_w(slice(2, 4), at_place(y1, place), dy=-1))
 
     def share_near(yy):
-        for first_place, count in ((0, 3), (6, 2)):
+        for first_place, count in ((0, 4), (5, 3)):
             rows = pl.ds(pl.multiple_of(yy * 256 + 32 * first_place, 32), 32 * count)
             s_sn.append(send_w(every, rows, core=sib))
 
@@ -244,16 +250,12 @@
         for k in range(2):
             for place, dz in ((up_place, 1), (down_place, -1)):
                 from_z[place, k].wait_recv()
-                if place not in (3, 5) or (place == 5) == (k == 0):
-                    from_z[(place - dz) % 8, k] = along_z(place, dz, halves[k])
+                from_z[(place - dz) % 8, k] = along_z(place, dz, halves[k])
 
     pass_on(7, 1)
     spread_near(7)
+    spread_near(1)
     relay_near(0)
-    fz = x * 4 + (1 - zh) * 2 + c
-    s_tz.wait_recv()
-    s_ty = [send(tab.at[fz, quarter], tab.at[fz, quarter], at(dy=k)) for k in (1, -1, 2)]
-    spread_near(1)
     f3, f1 = x3 * 4 + zh * 2 + c, x1 * 4 + zh * 2 + c
     s_tp.wait_recv()
     s_tm.wait_recv()
@@ -263,20 +265,27 @@
         send(tab.at[f3], tab.at[f3], at(core=sib)),
         send(tab.at[f1], tab.at[f1], at(core=sib)),
     ]
+    fz = x * 4 + (1 - zh) * 2 + c
+    s_tz.wait_recv()
+    s_ty = [send(tab.at[fz, quarter], tab.at[fz, quarter], at(dy=k)) for k in (1, -1, 2)]
     pass_on(6, 2)
     spread_near(6)
-    s_z = [across(0), across(1)]
-    spread_near(2)
+    s_z = [across(0)]
+    for copy in s_ss:
+        copy.wait_recv()
+    ssx[...] = ssp[x] + ssr[0] + ssr[1] + ssr[2]
+    s_ssz = send(ssx, ssz, at(dz=8))
+    s_z.append(across(1))
+    far_z[0].wait_recv()
+    s_wx = [send_w(x, far_rows(y), dx=k) for k in (1, -1, 2)]
     s_x = first_hop()
     for copy in s_ty:
         copy.wait_recv()
     s_uz = [send(tab.at[fz], tab.at[fz], at(dx=k)) for k in (2, 1, -1)]
     s_us = [send(tab.at[fz], tab.at[fz], at(core=sib))]
-    share_near(y)
-    pass_on(5, 3)
     relay_near(7)
+    spread_near(2)
     relay_near(1)
-    hops = second_hop()
 
     ids = codes[...]
     row = lax.broadcasted_iota(jnp.int32, (512, 64), 0)
@@ -291,24 +300,26 @@
     picked = jnp.where(lax.rem(row8, 8) == col8, high * 32.0 + low, 0.0)
     id_col = jnp.sum(picked, axis=1, keepdims=True).astype(jnp.int32)
 
-    for copy in s_ss:
-        copy.wait_recv()
-    ssx[...] = ssp[x] + ssr[0] + ssr[1] + ssr[2]
-    s_ssz = send(ssx, ssz, at(dz=8))
+    hops = second_hop()
     f2 = x2 * 4 + zh * 2 + c
     s_tx[0].wait_recv()
     s_tx[1].wait_recv()
     s_tx.append(send(tab.at[f2], tab.at[f2], at(core=sib)))
+    for place in (5, 3):
+        for k in range(2):
+            from_z[place, k].wait_recv()
+        spread_near(place)
     relay_near(6)
-    relay_near(2)
+    share_near(y)
+    spread_far(0)
+    for r in (1, 2, 3):
+        s_wx[r - 1].wait_recv()
+        spread_far(r)
     for copy, xx in zip(s_uz, (x2, x3, x1)):
         copy.wait_recv()
         ref = tab.at[xx * 4 + (1 - zh) * 2 + c]
         s_us.append(send(ref, ref, at(core=sib)))
-    from_z[4, 0].wait_recv()
-    from_z[4, 1].wait_recv()
-    spread_far(0)
-    spread_far(1)
+    relay_near(2)
     l_tab.wait()
     for copy in [s_ts] + s_tx[2:] + s_us:
         copy.wait_recv()
@@ -319,8 +330,10 @@
         onehot = (lanes == id_col[128 * t : 128 * (t + 1)]).astype(F32).astype(BF)
         emb[128 * t : 128 * (t + 1)] = dot(onehot, whole_table).astype(BF)
 
-    relay_far(0)
-    spread_far(2)
+    relay_near(5)
+    relay_near(3)
+    share_near(y1)
+    share_near(y3)
 
     for copy in s_x[2:] + hops:
         copy.wait_recv()
@@ -348,14 +361,14 @@
         for k in range(4):
             part_k = pltpu.roll(value[:, 256 * k : 256 * (k + 1)], turn, 1)
             normed[rows, 256 * k : 256 * (k + 1)] = part_k.astype(BF)
+    relay_far(0)
     relay_far(1)
-    spread_far(3)
     for copy in s_yn:
         copy.wait_recv()
-    for yy in (y1, y2, y3):
-        share_near(yy)
+    share_near(y2)
+    relay_far(2)
+    relay_far(3)
     finish_far(0)
-    relay_far(2)
     finish_far(1)
 
     first = lax.broadcasted_iota(jnp.int32, (128, 128), 1) < 64
@@ -408,18 +421,19 @@
     for copy in s_sn:
         copy.wait_recv()
     for r in range(4):
-        if r == 1:
-            finish_far(2)
-            relay_far(3)
-        if r == 2:
-            finish_far(3)
+        if 0 < r < 3:
+            finish_far(r + 1)
+        if r == 3:
+            for t in range(4):
+                rows = slice(128 * t, 128 * (t + 1))
+                stream[rows] = stream[rows] + dot(mixed[rows, :768], doutb[:768])
         for copy in s_ws[r]:
             copy.wait_recv()
         attend(r)
     stores = []
     for t in range(4):
         rows = slice(128 * t, 128 * (t + 1))
-        outb[rows] = (stream[rows] + dot(mixed[rows], doutb[...])).astype(BF)
+        outb[rows] = (stream[rows] + dot(mixed[rows, 768:], doutb[768:])).astype(BF)
         stores.append(load(outb.at[rows], out.at[rows]))
     for copy in stores:
         copy.wait()

time: 67.7 us -> 64.5 us (0.953)
  the two profiles are of different devices: /device:TPU:64 before, /device:TPU:1 now
where the time goes in v4:
time: 64.5 us; the launch traced here: 64.4 us
  Pallas kernels  63.4 us (98%)
  local copies, waits for them, and re-layouts  0.97 us (2%)
    pallas_call x1, Pallas kernels, per_device(): pl.pallas_call(kernel, out_shape=jax.ShapeDtypeStruct((512, 1024), BF), i...  63.4 us

profile of v4, /device:TPU:1, one launch (start us, length us, event | category | flops | bytes accessed | tf_op | source)
XLA Modules:
  0.0 64.4 jit_solution(4023439854667015341)
XLA Ops:
  0.0 63.4 %shard_map.82 = bf16[512,1024]{1,0:T(8,128)(2,1)S(1)} custom-call(bf16[4,2,2,64,256]{4,3,2,1,0:T(8,128)(2,1)} %bitcast.6, bf16[256]{0:T(256)(128)(2,1)} %gain.1, bf16[256,1024]{1,0:T(8,128)(2,1)} %proj.1, bf16[64,1024]{1,0:T(8,128)(2,1)} %table.1, bf16[1024]{0:T(1024)(128)(2,1)} %dgain.1, bf16[32,3072]{1,0:T(8,128)(2,1)} %dproj.1, bf16[1024,1024]{1,0:T(8,128)(2,1)} %dout.1, ...), custom_call_target="tpu_custom_call" | custom-call | flops 6499999744 | bytes 6000000 | tf_op jit(solution)/shard_map/pallas_call | solution.py:487
  63.4 1.0 %copy.10 = bf16[1,1,64,8,1024]{4,3,2,1,0:T(8,128)(2,1)} copy(bf16[1,1,64,8,1024]{4,3,2,1,0:T(8,128)(2,1)S(1)} %bitcast.5) | data formatting | bytes 2097152

commit v5 on v4

--- a/solution.py
+++ b/solution.py
@@ -25,7 +25,7 @@
     tbuf, pbuf, gbuf, pacc, part, rel, rx, stg, fx, zs, zf,
     ssp, ssr, ssx, ssz,
     tab, emb, normed, stream,
-    wb, qkv, comp, mixed, doutb, outb,
+    wb, early, qkv, comp, mixed, doutb, outb,
     ssem, rsem, lsem,
 ):
     fs = lax.axis_index("fsdp")
@@ -363,13 +363,32 @@
             normed[rows, 256 * k : 256 * (k + 1)] = part_k.astype(BF)
     relay_far(0)
     relay_far(1)
-    for copy in s_yn:
-        copy.wait_recv()
-    share_near(y2)
     relay_far(2)
     relay_far(3)
-    finish_far(0)
-    finish_far(1)
+
+    def columns(yy):
+        return pl.ds(pl.multiple_of(yy * 256, 256), 256)
+
+    def product(r, rows, yy):
+        return dot(normed[rows, columns(yy)], wb[ring[r], columns(yy)])
+
+    for copy in s_sn:
+        copy.wait_recv()
+    for r in range(4):
+        for copy in s_ws[r]:
+            copy.wait_recv()
+        for t in range(2):
+            rows = slice(256 * t, 256 * (t + 1))
+            early[r, rows] = product(r, rows, y) + product(r, rows, y1) + product(r, rows, y3)
+        if r == 0:
+            for copy in s_yn:
+                copy.wait_recv()
+            s_so = len(s_sn)
+            share_near(y2)
+    last = []
+    for r in range(4):
+        finish_far(r)
+        last.append(s_ws[r][-1])
 
     first = lax.broadcasted_iota(jnp.int32, (128, 128), 1) < 64
     frame_of_lane = lax.broadcasted_iota(jnp.int32, (8, 128), 1) // 8
@@ -385,7 +404,7 @@
     def attend(r):
         for t in range(2):
             rows = slice(256 * t, 256 * (t + 1))
-            qkv[rows] = dot(normed[rows], wb[ring[r]]).astype(BF)
+            qkv[rows] = (early[r, rows] + product(r, rows, y2)).astype(BF)
         for t in range(4):
             rows = slice(128 * t, 128 * (t + 1))
             for b in range(2):
@@ -418,17 +437,14 @@
 
     for copy in l_out:
         copy.wait()
-    for copy in s_sn:
+    for copy in s_sn[s_so:]:
         copy.wait_recv()
     for r in range(4):
-        if 0 < r < 3:
-            finish_far(r + 1)
+        last[r].wait_recv()
         if r == 3:
             for t in range(4):
                 rows = slice(128 * t, 128 * (t + 1))
                 stream[rows] = stream[rows] + dot(mixed[rows, :768], doutb[:768])
-        for copy in s_ws[r]:
-            copy.wait_recv()
         attend(r)
     stores = []
     for t in range(4):
@@ -468,6 +484,7 @@
         ((512, 1024), BF),
         ((512, 1024), F32),
         ((4, 1024, 768), BF),
+        ((4, 512, 768), F32),
         ((512, 768), BF),
         ((128, 128), F32),
         ((512, 1024), BF),
@@ -496,7 +513,7 @@
             pltpu.SemaphoreType.DMA((32,)),
         ],
         compiler_params=pltpu.CompilerParams(
-            collective_id=0, has_side_effects=True, vmem_limit_bytes=40 * 1024 * 1024
+            collective_id=0, has_side_effects=True, vmem_limit_bytes=44 * 1024 * 1024
         ),
         cost_estimate=pl.CostEstimate(
             flops=6_500_000_000, bytes_accessed=6_000_000, transcendentals=2_000_000

time: 64.5 us -> 62.4 us (0.967)
  Pallas kernels: 63.4 us -> 61.3 us
    pallas_call x1, Pallas kernels: 63.4 us -> 61.3 us  [per_device(): pl.pallas_call(kernel, out_shape=jax.ShapeDtypeStruct((512, 1024), BF), i...]
where the time goes in v5:
time: 62.4 us; the launch traced here: 62.3 us
  Pallas kernels  61.3 us (98%)
  local copies, waits for them, and re-layouts  0.97 us (2%)
    pallas_call x1, Pallas kernels, per_device(): pl.pallas_call(kernel, out_shape=jax.ShapeDtypeStruct((512, 1024), BF), i...  61.3 us

profile of v5, /device:TPU:1, one launch (start us, length us, event | category | flops | bytes accessed | tf_op | source)
XLA Modules:
  0.0 62.3 jit_solution(14471426097685985599)
XLA Ops:
  0.0 61.3 %shard_map.82 = bf16[512,1024]{1,0:T(8,128)(2,1)S(1)} custom-call(bf16[4,2,2,64,256]{4,3,2,1,0:T(8,128)(2,1)} %bitcast.6, bf16[256]{0:T(256)(128)(2,1)} %gain.1, bf16[256,1024]{1,0:T(8,128)(2,1)} %proj.1, bf16[64,1024]{1,0:T(8,128)(2,1)} %table.1, bf16[1024]{0:T(1024)(128)(2,1)} %dgain.1, bf16[32,3072]{1,0:T(8,128)(2,1)} %dproj.1, bf16[1024,1024]{1,0:T(8,128)(2,1)} %dout.1, ...), custom_call_target="tpu_custom_call" | custom-call | flops 6499999744 | bytes 6000000 | tf_op jit(solution)/shard_map/pallas_call | solution.py:504
  61.3 1.0 %copy.10 = bf16[1,1,64,8,1024]{4,3,2,1,0:T(8,128)(2,1)} copy(bf16[1,1,64,8,1024]{4,3,2,1,0:T(8,128)(2,1)S(1)} %bitcast.5) | data formatting | bytes 2097152

commit v6 on v5

--- a/solution.py
+++ b/solution.py
@@ -320,6 +320,7 @@
         ref = tab.at[xx * 4 + (1 - zh) * 2 + c]
         s_us.append(send(ref, ref, at(core=sib)))
     relay_near(2)
+    relay_near(5)
     l_tab.wait()
     for copy in [s_ts] + s_tx[2:] + s_us:
         copy.wait_recv()
@@ -330,7 +331,6 @@
         onehot = (lanes == id_col[128 * t : 128 * (t + 1)]).astype(F32).astype(BF)
         emb[128 * t : 128 * (t + 1)] = dot(onehot, whole_table).astype(BF)
 
-    relay_near(5)
     relay_near(3)
     share_near(y1)
     share_near(y3)

time: 62.4 us -> 62.5 us (level)
  no operation moved by 1% of the time
where the time goes in v6:
time: 62.5 us; the launch traced here: 62.4 us
  Pallas kernels  61.4 us (98%)
  local copies, waits for them, and re-layouts  0.97 us (2%)
    pallas_call x1, Pallas kernels, per_device(): pl.pallas_call(kernel, out_shape=jax.ShapeDtypeStruct((512, 1024), BF), i...  61.4 us

profile of v6, /device:TPU:1, one launch (start us, length us, event | category | flops | bytes accessed | tf_op | source)
XLA Modules:
  0.0 62.4 jit_solution(17956712665897487873)
XLA Ops:
  0.0 61.4 %shard_map.82 = bf16[512,1024]{1,0:T(8,128)(2,1)S(1)} custom-call(bf16[4,2,2,64,256]{4,3,2,1,0:T(8,128)(2,1)} %bitcast.6, bf16[256]{0:T(256)(128)(2,1)} %gain.1, bf16[256,1024]{1,0:T(8,128)(2,1)} %proj.1, bf16[64,1024]{1,0:T(8,128)(2,1)} %table.1, bf16[1024]{0:T(1024)(128)(2,1)} %dgain.1, bf16[32,3072]{1,0:T(8,128)(2,1)} %dproj.1, bf16[1024,1024]{1,0:T(8,128)(2,1)} %dout.1, ...), custom_call_target="tpu_custom_call" | custom-call | flops 6499999744 | bytes 6000000 | tf_op jit(solution)/shard_map/pallas_call | solution.py:504
  61.4 1.0 %copy.10 = bf16[1,1,64,8,1024]{4,3,2,1,0:T(8,128)(2,1)} copy(bf16[1,1,64,8,1024]{4,3,2,1,0:T(8,128)(2,1)S(1)} %bitcast.5) | data formatting | bytes 2097152
